TPU v7x, 32 devices: a whole 2x2x4 slice. The times are simulated.
32 devices in a mesh: dp: 8 (over z, x), ctx: 4 (over y, core).
Axes of the slice: x: 2, y: 2, z: 4, core: 2. Of those that a mesh axis runs over, the one named last changes fastest.
Arguments:
- inputs: bfloat16 [8192, 768], P(('dp', 'ctx')), may hold values from -8 to 8
- cotangent: bfloat16 [8192, 768], P(('dp', 'ctx')), may hold values from -6 to 6
- norm_gain: bfloat16 [2, 768], P(None, ('dp', 'ctx')), may hold values from 0.5 to 1.5
- proj_weight: bfloat16 [2, 768, 3328], P(None, ('dp', 'ctx')), may hold values from -0.21875 to 0.21875
- step_weight: bfloat16 [2, 768, 24], P(None, ('dp', 'ctx')), may hold values from -0.21875 to 0.21875
- conv_weight: bfloat16 [2, 4, 1792], P(None, None, ('dp', 'ctx')), may hold values from -3 to 3
- conv_bias: bfloat16 [2, 1792], P(None, ('dp', 'ctx')), may hold values from -1.5 to 1.5
- gate_gain: bfloat16 [2, 1536], P(None, ('dp', 'ctx')), may hold values from 0.5 to 1.5
- out_weight: bfloat16 [2, 1536, 768], P(None, ('dp', 'ctx')), may hold values from -0.15625 to 0.15625
- step_bias: float32 [2, 24], replicated, may hold values from -4 to -1
- decay_log: float32 [2, 24], replicated, may hold values from -4 to 0.5
- skip_scale: float32 [2, 24], replicated, may hold values from 0.5 to 1.5
Outputs:
- outputs: bfloat16 [8192, 768], P(('dp', 'ctx'))
- input_grad: float32 [8192, 768], P(('dp', 'ctx'))
- norm_gain_grad: float32 [2, 768], P(None, ('dp', 'ctx'))
- proj_weight_grad: float32 [2, 768, 3328], P(None, ('dp', 'ctx'))
- step_weight_grad: float32 [2, 768, 24], P(None, ('dp', 'ctx'))
- conv_weight_grad: float32 [2, 4, 1792], P(None, None, ('dp', 'ctx'))
- conv_bias_grad: float32 [2, 1792], P(None, ('dp', 'ctx'))
- gate_gain_grad: float32 [2, 1536], P(None, ('dp', 'ctx'))
- out_weight_grad: float32 [2, 1536, 768], P(None, ('dp', 'ctx'))
- step_bias_grad: float32 [2, 24], replicated
- decay_log_grad: float32 [2, 24], replicated
- skip_scale_grad: float32 [2, 24], replicated
All inputs are finite; a program needn't handle non-finite values.
Results may differ from a plain program's by a relative error of at most 0.025.
Values may be sent and summed in bfloat16 or wider, within the bound.
A program may use at most 192 MiB of HBM per device.

v0:
```python
import jax
import jax.numpy as jnp
from jax import lax
from jax.sharding import PartitionSpec as P

HEADS = 24
HDIM = 64
STATE = 128
CONV = 4
GROUP = 256
LAYERS = 2
INNER = 1536


EPSILON = 1e-05


def passed_along(block, axis, distance):
    devices = range(lax.axis_size(axis))
    route = [(i - distance, i) for i in devices if i - distance in devices]
    return lax.ppermute(block, axis, route)


def prefix(array, axis, combine, identity, reverse):
    peers, place = (lax.axis_size(axis), lax.axis_index(axis))
    everything = jax.tree.map(
        lambda part, kind: lax.all_gather(part.astype(kind), axis),
        array,
        (jnp.bfloat16, jnp.bfloat16),
    )
    start = jax.tree.map(
        lambda part, zero: jnp.broadcast_to(jnp.asarray(zero, part.dtype), part.shape),
        array,
        identity,
    )

    def hop(k, before):
        at = peers - 1 - k if reverse else k
        reached = at > place if reverse else at < place
        new = combine(
            before, jax.tree.map(lambda part, own: part[at].astype(own.dtype), everything, array)
        )
        return jax.tree.map(lambda a, b: jnp.where(reached, a, b), new, before)

    return lax.fori_loop(0, peers, hop, start)


def rms_scale(values, gain):
    return values * lax.rsqrt(jnp.mean(values * values, axis=-1, keepdims=True) + EPSILON) * gain


def gated_norm(values, gate_in, gain):
    return rms_scale(values * jax.nn.silu(gate_in), gain)


def conv_act(extended, kernel, offset):
    row_count = extended.shape[0] - (CONV - 1)
    summed = offset
    for tap_index in range(CONV):
        summed = summed + kernel[tap_index] * extended[tap_index : tap_index + row_count]
    return jax.nn.silu(summed)


def rates(step_raw, step_bias, decay_log):
    step_size = jax.nn.softplus(step_raw + step_bias)
    return (-step_size * jnp.exp(decay_log), step_size)


def decays(scores, decay_rate, step_size):
    cumulative = jnp.cumsum(decay_rate, axis=1)
    block_total = cumulative[:, -1]
    block_width = decay_rate.shape[1]
    causal = jnp.arange(block_width)[:, None] >= jnp.arange(block_width)[None, :]
    cum_heads = jnp.swapaxes(cumulative, 1, 2)
    difference = cum_heads[:, :, :, None] - cum_heads[:, :, None, :]
    kernel = jnp.where(causal, jnp.exp(jnp.where(causal, difference, 0.0)), 0.0)
    mixing = scores[:, None] * kernel * jnp.swapaxes(step_size, 1, 2)[:, :, None, :]
    weight = jnp.exp(block_total[:, None, :] - cumulative) * step_size
    growth = jnp.exp(cumulative)
    return (mixing, weight, growth, block_total)


def advance(state_now, inputs_pair):
    shrink_log, fresh_state = inputs_pair
    return (jnp.exp(shrink_log)[:, None, None] * state_now + fresh_state, state_now)


def retreat(later_grad, inputs_pair):
    shrink_log, direct = inputs_pair
    return (direct + jnp.exp(shrink_log)[:, None, None] * later_grad, later_grad)


def combine(earlier, later_part):
    return (earlier[0] * later_part[0], earlier[1] * later_part[0][:, None, None] + later_part[1])


def contract_rows(left_side, right_side):
    return lax.dot_general(
        left_side, right_side, (((0,), (0,)), ((), ())), preferred_element_type=jnp.float32
    )


def contract_cols(left_side, right_side):
    return lax.dot_general(
        left_side, right_side, (((1,), (1,)), ((), ())), preferred_element_type=jnp.float32
    )


def forward_layer(hidden, params, head_params):
    gain_in, proj_w, rate_w, kernel, offset, gain_out, out_w = params
    step_bias, decay_log, skip_scale = head_params
    row_count = hidden.shape[0]
    groups = row_count // GROUP
    scaled_in, pull_norm = jax.vjp(rms_scale, hidden, gain_in.astype(jnp.float32))
    normed = scaled_in.astype(jnp.bfloat16)
    projected = jnp.dot(normed, proj_w, preferred_element_type=jnp.float32)
    step_raw = jnp.dot(normed, rate_w, preferred_element_type=jnp.float32)
    gate_in = projected[:, :INNER]
    conv_in = projected[:, INNER:]
    edge_rows = passed_along(conv_in[row_count - (CONV - 1) :], "ctx", 1)
    extended = jnp.concatenate([edge_rows, conv_in], 0)
    act, pull_conv = jax.vjp(
        conv_act, extended, kernel.astype(jnp.float32), offset.astype(jnp.float32)
    )
    values = act[:, :INNER].astype(jnp.bfloat16).reshape(groups, GROUP, HEADS, HDIM)
    write_keys = act[:, INNER : INNER + STATE].astype(jnp.bfloat16).reshape(groups, GROUP, STATE)
    read_keys = act[:, INNER + STATE :].astype(jnp.bfloat16).reshape(groups, GROUP, STATE)
    (decay_rate, step_size), pull_rate = jax.vjp(rates, step_raw, step_bias, decay_log)
    scores = jnp.einsum("ctn,csn->cts", read_keys, write_keys, preferred_element_type=jnp.float32)
    (mixing, weight, growth, block_total), pull_decay = jax.vjp(
        decays,
        scores,
        decay_rate.reshape(groups, GROUP, HEADS),
        step_size.reshape(groups, GROUP, HEADS),
    )
    mixing_low = mixing.astype(jnp.bfloat16)
    diagonal = jnp.einsum("chts,cshp->cthp", mixing_low, values, preferred_element_type=jnp.float32)
    scaled = (values.astype(jnp.float32) * weight[..., None]).astype(jnp.bfloat16)
    update = jnp.einsum("cshp,csn->chpn", scaled, write_keys, preferred_element_type=jnp.float32)
    empty_state = jnp.zeros((HEADS, HDIM, STATE), jnp.float32)
    local_end, _ = lax.scan(advance, empty_state, (block_total, update))
    device_decay = jnp.exp(jnp.sum(block_total, axis=0))
    incoming = prefix(
        (device_decay, local_end), "ctx", combine, (jnp.ones_like(device_decay), empty_state), False
    )[1]
    _, states = lax.scan(advance, incoming, (block_total, update))
    held_low = states.astype(jnp.bfloat16)
    carried = jnp.einsum("ctn,chpn->cthp", read_keys, held_low, preferred_element_type=jnp.float32)
    mixed_out = (
        diagonal + growth[..., None] * carried + skip_scale[:, None] * values.astype(jnp.float32)
    )
    mixed_out = mixed_out.reshape(row_count, INNER)
    normed_float, pull_gate = jax.vjp(gated_norm, mixed_out, gate_in, gain_out.astype(jnp.float32))
    normed_out = normed_float.astype(jnp.bfloat16)
    branch = jnp.dot(normed_out, out_w, preferred_element_type=jnp.float32)
    kept_values = (
        normed,
        pull_norm,
        pull_conv,
        pull_rate,
        pull_decay,
        values,
        write_keys,
        read_keys,
        mixing_low,
        scaled,
        states,
        held_low,
        carried,
        growth,
        weight,
        block_total,
        device_decay,
        pull_gate,
        normed_out,
    )
    return (hidden + branch, kept_values)


def backward_layer(grad_hidden, params, head_params, kept_values):
    gain_in, proj_w, rate_w, kernel, offset, gain_out, out_w = params
    skip_scale = head_params[2]
    (
        normed,
        pull_norm,
        pull_conv,
        pull_rate,
        pull_decay,
        values,
        write_keys,
        read_keys,
        mixing_low,
        scaled,
        states,
        held_low,
        carried,
        growth,
        weight,
        block_total,
        device_decay,
        pull_gate,
        normed_out,
    ) = kept_values
    row_count = grad_hidden.shape[0]
    groups = row_count // GROUP
    grad_branch = grad_hidden.astype(jnp.bfloat16)
    out_grad = contract_rows(normed_out, grad_branch)
    grad_normed = contract_cols(grad_branch, out_w)
    grad_mixed, grad_gate, gain_out_grad = pull_gate(grad_normed)
    grad_y = grad_mixed.astype(jnp.bfloat16).reshape(groups, GROUP, HEADS, HDIM)
    grad_float = grad_y.astype(jnp.float32)
    grad_mixing = jnp.einsum("cthp,cshp->chts", grad_y, values, preferred_element_type=jnp.float32)
    grad_values = jnp.einsum(
        "chts,cthp->cshp", mixing_low, grad_y, preferred_element_type=jnp.float32
    )
    grad_values = grad_values + skip_scale[:, None] * grad_float
    skip_grad = jnp.sum(grad_float * values, axis=(0, 1, 3))
    grad_growth = jnp.sum(grad_float * carried, axis=-1)
    grad_carried = (growth[..., None] * grad_float).astype(jnp.bfloat16)
    grad_read = jnp.einsum(
        "cthp,chpn->ctn", grad_carried, held_low, preferred_element_type=jnp.float32
    )
    grad_held = jnp.einsum(
        "cthp,ctn->chpn", grad_carried, read_keys, preferred_element_type=jnp.float32
    )
    empty_state = jnp.zeros((HEADS, HDIM, STATE), jnp.float32)
    local_start, _ = lax.scan(retreat, empty_state, (block_total, grad_held), reverse=True)
    outgoing = prefix(
        (device_decay, local_start),
        "ctx",
        combine,
        (jnp.ones_like(device_decay), empty_state),
        True,
    )[1]
    _, after_grad = lax.scan(retreat, outgoing, (block_total, grad_held), reverse=True)
    grad_total = jnp.exp(block_total) * jnp.sum(after_grad * states, axis=(2, 3))
    grad_update = after_grad.astype(jnp.bfloat16)
    grad_scaled = jnp.einsum(
        "chpn,csn->cshp", grad_update, write_keys, preferred_element_type=jnp.float32
    )
    grad_write = jnp.einsum(
        "chpn,cshp->csn", grad_update, scaled, preferred_element_type=jnp.float32
    )
    grad_values = grad_values + grad_scaled * weight[..., None]
    grad_weight = jnp.sum(grad_scaled * values, axis=-1)
    grad_scores, grad_rate, grad_step = pull_decay(
        (grad_mixing, grad_weight, grad_growth, grad_total)
    )
    grad_scores_low = grad_scores.astype(jnp.bfloat16)
    grad_read = grad_read + jnp.einsum(
        "cts,csn->ctn", grad_scores_low, write_keys, preferred_element_type=jnp.float32
    )
    grad_write = grad_write + jnp.einsum(
        "cts,ctn->csn", grad_scores_low, read_keys, preferred_element_type=jnp.float32
    )
    grad_raw, bias_grad, decay_grad = pull_rate(
        (grad_rate.reshape(row_count, HEADS), grad_step.reshape(row_count, HEADS))
    )
    grad_act = jnp.concatenate(
        [
            grad_values.reshape(row_count, INNER),
            grad_write.reshape(row_count, STATE),
            grad_read.reshape(row_count, STATE),
        ],
        1,
    )
    grad_extended, kernel_grad, offset_grad = pull_conv(grad_act)
    back_edge = passed_along(grad_extended[: CONV - 1], "ctx", -1)
    grad_conv_in = grad_extended[CONV - 1 :] + jnp.pad(
        back_edge, ((row_count - (CONV - 1), 0), (0, 0))
    )
    grad_projected = jnp.concatenate([grad_gate, grad_conv_in], 1).astype(jnp.bfloat16)
    grad_raw_low = grad_raw.astype(jnp.bfloat16)
    proj_grad = contract_rows(normed, grad_projected)
    rate_grad = contract_rows(normed, grad_raw_low)
    grad_normed_in = contract_cols(grad_projected, proj_w) + contract_cols(grad_raw_low, rate_w)
    grad_input, gain_in_grad = pull_norm(grad_normed_in)
    weight_grads = (
        gain_in_grad,
        proj_grad,
        rate_grad,
        jnp.transpose(kernel_grad),
        offset_grad,
        gain_out_grad,
        out_grad,
    )
    return (grad_hidden + grad_input, weight_grads, (bias_grad, decay_grad, skip_grad))


def on_device(
    inputs,
    cotangent,
    norm_gain,
    proj_weight,
    step_weight,
    conv_weight,
    conv_bias,
    gate_gain,
    out_weight,
    step_bias,
    decay_log,
    skip_scale,
):
    gathered = (
        lax.all_gather(norm_gain, ("dp", "ctx"), axis=1, tiled=True),
        lax.all_gather(proj_weight, ("dp", "ctx"), axis=1, tiled=True),
        lax.all_gather(step_weight, ("dp", "ctx"), axis=1, tiled=True),
        lax.all_gather(conv_weight, ("dp", "ctx"), axis=2, tiled=True),
        lax.all_gather(conv_bias, ("dp", "ctx"), axis=1, tiled=True),
        lax.all_gather(gate_gain, ("dp", "ctx"), axis=1, tiled=True),
        lax.all_gather(out_weight, ("dp", "ctx"), axis=1, tiled=True),
    )
    hidden = inputs.astype(jnp.float32)
    saved_list = []
    for layer_index in range(LAYERS):
        params = tuple((member[layer_index] for member in gathered))
        head_params = (step_bias[layer_index], decay_log[layer_index], skip_scale[layer_index])
        hidden, kept_values = forward_layer(hidden, params, head_params)
        saved_list.append(kept_values)
    outputs = hidden.astype(jnp.bfloat16)
    gathered = (
        lax.all_gather(norm_gain, ("dp", "ctx"), axis=1, tiled=True),
        lax.all_gather(proj_weight, ("dp", "ctx"), axis=1, tiled=True),
        lax.all_gather(step_weight, ("dp", "ctx"), axis=1, tiled=True),
        lax.all_gather(conv_weight, ("dp", "ctx"), axis=2, tiled=True),
        lax.all_gather(conv_bias, ("dp", "ctx"), axis=1, tiled=True),
        lax.all_gather(gate_gain, ("dp", "ctx"), axis=1, tiled=True),
        lax.all_gather(out_weight, ("dp", "ctx"), axis=1, tiled=True),
    )
    grad_hidden = cotangent.astype(jnp.float32)
    layer_weight_grads = [None] * LAYERS
    layer_head_grads = [None] * LAYERS
    for layer_index in reversed(range(LAYERS)):
        params = tuple((member[layer_index] for member in gathered))
        head_params = (step_bias[layer_index], decay_log[layer_index], skip_scale[layer_index])
        grad_hidden, weight_grads, head_grads = backward_layer(
            grad_hidden, params, head_params, saved_list[layer_index]
        )
        layer_weight_grads[layer_index] = tuple(weight_grads)
        layer_head_grads[layer_index] = head_grads
    flat_grads = tuple(
        (member for layer_index in range(LAYERS) for member in layer_weight_grads[layer_index])
    )
    flat_grads = lax.psum_scatter(flat_grads, ("dp", "ctx"), scatter_dimension=0, tiled=True)
    stacked = [
        jnp.stack([flat_grads[layer_index * 7 + member] for layer_index in range(LAYERS)])
        for member in range(7)
    ]
    gain_in_all, proj_all, rate_all, kernel_all, offset_all, gain_out_all, out_all = stacked
    kernel_all = jnp.swapaxes(kernel_all, 1, 2)
    bias_all = jnp.stack([layer_head_grads[layer_index][0] for layer_index in range(LAYERS)])
    decay_all = jnp.stack([layer_head_grads[layer_index][1] for layer_index in range(LAYERS)])
    skip_all = jnp.stack([layer_head_grads[layer_index][2] for layer_index in range(LAYERS)])
    bias_all, decay_all, skip_all = lax.psum((bias_all, decay_all, skip_all), ("dp", "ctx"))
    return (
        outputs,
        grad_hidden,
        gain_in_all,
        proj_all,
        rate_all,
        kernel_all,
        offset_all,
        gain_out_all,
        out_all,
        bias_all,
        decay_all,
        skip_all,
    )


def solution(mesh):
    in_specs = (
        P(("dp", "ctx"), None),
        P(("dp", "ctx"), None),
        P(None, ("dp", "ctx")),
        P(None, ("dp", "ctx"), None),
        P(None, ("dp", "ctx"), None),
        P(None, None, ("dp", "ctx")),
        P(None, ("dp", "ctx")),
        P(None, ("dp", "ctx")),
        P(None, ("dp", "ctx"), None),
        P(),
        P(),
        P(),
    )
    out_specs = (
        P(("dp", "ctx"), None),
        P(("dp", "ctx"), None),
        P(None, ("dp", "ctx")),
        P(None, ("dp", "ctx"), None),
        P(None, ("dp", "ctx"), None),
        P(None, None, ("dp", "ctx")),
        P(None, ("dp", "ctx")),
        P(None, ("dp", "ctx")),
        P(None, ("dp", "ctx"), None),
        P(),
        P(),
        P(),
    )
    return jax.shard_map(
        on_device, mesh=mesh, in_specs=in_specs, out_specs=out_specs, check_vma=False
    )
```

profile of v0, /device:TPU:0, one launch (start us, length us, event | category | flops | bytes accessed | tf_op | source)
XLA Modules:
  0.0 1427.9 jit_solution(9335978089923642418)
XLA Ops:
  8.0 43.4 %all-gather.7 = bf16[32,24,2]{1,2,0:T(2,128)(2,1)S(1)} all-gather(bf16[1,24,2]{1,2,0:T(2,128)(2,1)} %bitcast.592), channel_id=1, replica_groups=mesh['dp'=8,'ctx'=4] {'dp','ctx'}, dimensions={0}, use_global_device_ids=true | all-gather | bytes 3168 | tf_op jit(solution)/shard_map/all_gather | solution.py:305
  52.2 36.9 %all-gather.6 = bf16[32,56,2]{1,2,0:T(2,128)(2,1)S(1)} all-gather(bf16[1,56,2]{1,2,0:T(2,128)(2,1)} %bitcast.593), channel_id=1, replica_groups=mesh['dp'=8,'ctx'=4] {'dp','ctx'}, dimensions={0}, use_global_device_ids=true | all-gather | bytes 7392 | tf_op jit(solution)/shard_map/all_gather | solution.py:309
  89.3 39.6 %all_gather.56 = bf16[2,768,24]{2,1,0:T(8,128)(2,1)S(1)} all-gather(bf16[2,24,24]{2,1,0:T(8,128)(2,1)} %param.25), channel_id=1, replica_groups=mesh['dp'=8,'ctx'=4] {'dp','ctx'}, dimensions={1}, use_global_device_ids=true | all-gather | bytes 76032 | tf_op jit(solution)/shard_map/all_gather | solution.py:307
  136.7 39.3 %all_gather.53 = bf16[2,4,1792]{1,0,2:T(2,128)(2,1)S(1)} all-gather(bf16[2,4,56]{1,0,2:T(2,128)(2,1)S(1)} %copy.348), channel_id=1, replica_groups=mesh['dp'=8,'ctx'=4] {'dp','ctx'}, dimensions={2}, use_global_device_ids=true | all-gather | bytes 29568 | tf_op jit(solution)/shard_map/all_gather | solution.py:308
  178.5 37.5 %slice_reduce_fusion.7 = (f32[1792]{0:T(1024)S(1)}, f32[1792]{0:T(1024)S(1)}, f32[1792]{0:T(1024)S(1)}, f32[1792]{0:T(1024)S(1)}) fusion(f32[1,4,1792]{1,0,2:T(1,128)S(1)} %get-tuple-element.782), kind=kLoop, calls=%fused_computation.169 | loop fusion | bytes 57344 | tf_op jit(solution)/shard_map/jvp()/slice | solution.py:60
  235.0 5.2 all-gather
  241.1 37.7 %all-gather.8 = bf16[32,48,2]{1,2,0:T(2,128)(2,1)S(1)} all-gather(bf16[1,48,2]{1,2,0:T(2,128)(2,1)S(1)} %bitcast.594), channel_id=1, replica_groups=mesh['dp'=8,'ctx'=4] {'dp','ctx'}, dimensions={0}, use_global_device_ids=true | all-gather | bytes 6336 | tf_op jit(solution)/shard_map/all_gather | solution.py:310
  279.6 37.7 %slice_reduce_fusion.3 = (f32[1792]{0:T(1024)}, f32[1792]{0:T(1024)}, f32[1792]{0:T(1024)}, f32[1792]{0:T(1024)}) fusion(f32[1,4,1792]{1,0,2:T(1,128)S(1)} %get-tuple-element.781), kind=kLoop, calls=%fused_computation.164 | loop fusion | bytes 57344 | tf_op jit(solution)/shard_map/jvp()/slice | solution.py:60
  374.6 5.1 all-gather.2
  437.0 7.1 fusion.13
  472.4 5.2 fusion.41
  492.9 5.1 multiply_reduce_fusion.24
  515.0 6.8 fusion.15
  527.6 5.0 while.43
  570.3 5.6 fusion.59
  588.3 6.6 fusion.55
  596.2 6.5 fusion.54
  608.4 93.6 %all-reduce.33.cloned.1.call-done = (f32[768]{0:T(1024)}, f32[768]{0:T(1024)}, f32[1792,4]{0,1:T(4,128)}, f32[1792,4]{0,1:T(4,128)}, f32[1792]{0:T(1024)}, /*ind...) async-done(((f32[768]{0:T(1024)}, f32[768]{0:T(1024)}, f32[1792,4]{0,1:T(4,128)}, ...) | async-done | bytes 90704
  707.5 96.5 %reduce-scatter.23.cloned.1.call-done = f32[24,24]{1,0:T(8,128)} async-done(((f32[768,24]{1,0:T(8,128)}), f32[24,24]{1,0:T(8,128)}) %reduce-scatter.23.cloned.1.call-update) | async-done | bytes 2320
  804.0 98.8 %reduce-scatter.21.cloned.1.call-done = f32[24,24]{1,0:T(8,128)} async-done(((f32[768,24]{1,0:T(8,128)}), f32[24,24]{1,0:T(8,128)}) %reduce-scatter.21.cloned.1.call-update) | async-done | bytes 2320
  904.2 111.0 %reduce-scatter.19.cloned.1.call-done = f32[48,768]{1,0:T(8,128)} async-done(((f32[1536,768]{1,0:T(8,128)}), f32[48,768]{1,0:T(8,128)}) %reduce-scatter.19.cloned.1.call-update) | async-done | bytes 147472 | tf_op jit(solution)/shard_map/reduce_scatter | solution.py:344
  1015.2 111.6 %reduce-scatter.17.cloned.1.call-done = f32[48,768]{1,0:T(8,128)} async-done(((f32[1536,768]{1,0:T(8,128)}), f32[48,768]{1,0:T(8,128)}) %reduce-scatter.17.cloned.1.call-update) | async-done | bytes 147472 | tf_op jit(solution)/shard_map/reduce_scatter | solution.py:344
  1128.5 143.5 %reduce-scatter.15.cloned.1.call-done = f32[24,3328]{1,0:T(8,128)} async-done(((f32[768,3328]{1,0:T(8,128)}), f32[24,3328]{1,0:T(8,128)}) %reduce-scatter.15.cloned.1.call-update) | async-done | bytes 319504 | tf_op jit(solution)/shard_map/reduce_scatter | solution.py:344
  1272.1 145.5 %reduce-scatter.13.cloned.1.call-done = f32[24,3328]{1,0:T(8,128)} async-done(((f32[768,3328]{1,0:T(8,128)}), f32[24,3328]{1,0:T(8,128)}) %reduce-scatter.13.cloned.1.call-update) | async-done | bytes 319504 | tf_op jit(solution)/shard_map/reduce_scatter | solution.py:344
  (648 shorter events, 300.1 us)
Async XLA Ops:
  7.2 208.9 %all-gather.16.cloned.1.call-start = ((), (), s32[]{:S(2)}) async-start(), calls=%async_computation.6 | async-start | bytes 10543104 | tf_op jit(solution)/shard_map/all_gather | solution.py:306
  7.9 313.8 %all-gather.20.cloned.1.call-start = ((), (), s32[]{:S(2)}) async-start(), calls=%async_computation.12 | async-start | bytes 1966080 | tf_op jit(solution)/shard_map/all_gather | solution.py:27
  221.9 6.3 collective-permute-start
  233.5 103.9 %all-gather.18.cloned.1.call-start = ((), (), s32[]{:S(2)}) async-start(), calls=%async_computation.7 | async-start | bytes 4866048 | tf_op jit(solution)/shard_map/all_gather | solution.py:311
  234.2 158.9 %all-gather.22.cloned.1.call-start = ((), (), s32[]{:S(2)}) async-start(), calls=%async_computation.13 | async-start | bytes 1966080 | tf_op jit(solution)/shard_map/all_gather | solution.py:27
  240.9 86.2 %copy-start.125 = (f32[24,256]{1,0:T(8,128)}, f32[24,256]{1,0:T(8,128)S(1)}, u32[]{:S(2)}) copy-start(f32[24,256]{1,0:T(8,128)S(1)} %copy.355) | copy-start | bytes 73732
  241.1 86.0 %copy-start.93 = (f32[256,24]{0,1:T(8,128)}, f32[256,24]{0,1:T(8,128)S(1)}, u32[]{:S(2)}) copy-start(f32[256,24]{0,1:T(8,128)S(1)} %copy.357) | copy-start | bytes 73732
  279.0 58.9 %copy-start.107 = (f32[1536]{0:T(1024)}, f32[1536]{0:T(1024)S(1)}, u32[]{:S(2)}) copy-start(f32[1536]{0:T(1024)S(1)} %get-tuple-element.693) | copy-start | bytes 18436
  350.2 13.8 collective-permute-start.1
  373.8 77.3 %all-gather.24.cloned.1.call-start = ((), (), s32[]{:S(2)}) async-start(), calls=%async_computation.14 | async-start | bytes 1966080 | tf_op jit(solution)/shard_map/all_gather | solution.py:27
  380.7 56.3 %copy-start.127 = (f32[24,256]{1,0:T(8,128)}, f32[24,256]{1,0:T(8,128)S(1)}, u32[]{:S(2)}) copy-start(f32[24,256]{1,0:T(8,128)S(1)} %copy.369) | copy-start | bytes 73732
  425.0 102.6 %all-gather.26.cloned.1.call-start = ((), (), s32[]{:S(2)}) async-start(), calls=%async_computation.15 | async-start | bytes 1966080 | tf_op jit(solution)/shard_map/all_gather | solution.py:27
  488.0 3.1 collective-permute-start.2
  508.7 193.4 %all-reduce.33.cloned.1.call-start = ((), (), s32[]{:S(2)}) async-start(), calls=%async_computation.18 | async-start | bytes 202752
  562.5 5.1 collective-permute-start.3
  575.9 228.2 %reduce-scatter.23.cloned.1.call-start = ((), (), s32[]{:S(2)}) async-start(), calls=%async_computation.17 | async-start | bytes 405504
  577.0 325.9 %reduce-scatter.21.cloned.1.call-start = ((), (), s32[]{:S(2)}) async-start(), calls=%async_computation.16 | async-start | bytes 405504
  578.2 437.0 %reduce-scatter.19.cloned.1.call-start = ((), (), s32[]{:S(2)}) async-start(), calls=%async_computation.11 | async-start | bytes 4866048 | tf_op jit(solution)/shard_map/reduce_scatter | solution.py:344
  581.5 545.3 %reduce-scatter.17.cloned.1.call-start = ((), (), s32[]{:S(2)}) async-start(), calls=%async_computation.10 | async-start | bytes 4866048 | tf_op jit(solution)/shard_map/reduce_scatter | solution.py:344
  587.1 685.0 %reduce-scatter.15.cloned.1.call-start = ((), (), s32[]{:S(2)}) async-start(), calls=%async_computation.9 | async-start | bytes 10543104 | tf_op jit(solution)/shard_map/reduce_scatter | solution.py:344
  594.9 822.6 %reduce-scatter.13.cloned.1.call-start = ((), (), s32[]{:S(2)}) async-start(), calls=%async_computation.8 | async-start | bytes 10543104 | tf_op jit(solution)/shard_map/reduce_scatter | solution.py:344
  702.1 717.4 %copy-start.169 = (f32[2,24]{1,0:T(2,128)S(1)}, f32[2,24]{1,0:T(2,128)}, u32[]{:S(2)}) copy-start(f32[2,24]{1,0:T(2,128)} %get-tuple-element.1056) | copy-start | bytes 580
  702.1 717.9 %copy-start.168 = (f32[2,24]{1,0:T(2,128)S(1)}, f32[2,24]{1,0:T(2,128)}, u32[]{:S(2)}) copy-start(f32[2,24]{1,0:T(2,128)} %get-tuple-element.1057) | copy-start | bytes 580
  702.1 718.5 %copy-start.167 = (f32[2,24]{1,0:T(2,128)S(1)}, f32[2,24]{1,0:T(2,128)}, u32[]{:S(2)}) copy-start(f32[2,24]{1,0:T(2,128)} %get-tuple-element.1058) | copy-start | bytes 580
  (169 other events, 1005.9 us)
Sparse Core Ops, SparseCore 0:
  10.9 89.9 all-gather.15
  233.6 17.2 all-gather.19
  253.7 63.6 all-gather.17
  373.9 15.5 all-gather.21
  425.1 15.9 all-gather.23
  508.8 17.9 all-gather.25
  576.0 126.0 all-reduce.32
  708.4 95.5 reduce-scatter.22
  809.0 93.8 reduce-scatter.20
  909.1 106.0 reduce-scatter.18
  1020.7 106.0 reduce-scatter.16
  1133.7 138.3 reduce-scatter.14
  1279.1 138.3 reduce-scatter.12
where the time goes:
time: 1430 us
  waiting for transfers between devices  804 us (56%)
  blocking collectives  207 us (14%)
  local copies, waits for them, and re-layouts  179 us (13%)
  matrix products  110 us (8%)
  other arithmetic  102 us (7%)
  between operations  16.1 us (1%)
    reduce_scatter x4, waiting for transfers between devices, on_device(): lax.psum_scatter(flat_grads, ('dp', 'ctx'), scatter_dimension=0, tiled=True)  512 us
    unnamed x16, waiting for transfers between devices  291 us
    slice x2, local copies, waits for them, and re-layouts, conv_act(): kernel[tap_index] * extended[tap_index:tap_index + row_count]  75.2 us
    all_gather x1, blocking collectives, on_device(): lax.all_gather(norm_gain, ('dp', 'ctx'), axis=1, tiled=True)  43.4 us
    all_gather x1, blocking collectives, on_device(): lax.all_gather(step_weight, ('dp', 'ctx'), axis=1, tiled=True)  39.6 us
    all_gather x1, blocking collectives, on_device(): lax.all_gather(conv_weight, ('dp', 'ctx'), axis=2, tiled=True)  39.3 us
    all_gather x1, blocking collectives, on_device(): lax.all_gather(gate_gain, ('dp', 'ctx'), axis=1, tiled=True)  37.7 us
    all_gather x1, blocking collectives, on_device(): lax.all_gather(conv_bias, ('dp', 'ctx'), axis=1, tiled=True)  36.9 us
  transfers between devices with their start and end apart: 17, of which 9 were waited for; matrix products, arithmetic and copies ran while one was open for 15% of the time, Pallas kernels for 0%

commit v1 on v0

v1 whole, which is shorter than its diff:
```python
import jax
import jax.numpy as jnp
from jax import lax
from jax.sharding import PartitionSpec as P

HEADS = 24
HDIM = 64
STATE = 128
CONV = 4
GROUP = 256
LAYERS = 2
INNER = 1536
CHANNELS = INNER + 2 * STATE
EXTRA = 128


EPSILON = 1e-05


def passed_along(block, axis, distance):
    devices = range(lax.axis_size(axis))
    route = [(i - distance, i) for i in devices if i - distance in devices]
    return lax.ppermute(block, axis, route)


AXES = ("dp", "ctx")


def swap_with(block, bit):
    count = lax.axis_size(AXES)
    return lax.ppermute(block, AXES, [(i, i ^ (1 << bit)) for i in range(count)])


def bit_orders():
    ctx_bits = lax.axis_size("ctx").bit_length() - 1
    all_bits = (lax.axis_size(AXES)).bit_length() - 1
    y_bits = list(range(1, ctx_bits))
    x_bits = [ctx_bits]
    z_bits = list(range(ctx_bits + 1, all_bits))
    return ([0] + y_bits + x_bits + z_bits, [0] + x_bits + z_bits + y_bits, [0] + z_bits + y_bits + x_bits)


def side(bit):
    return lax.rem(lax.div(lax.axis_index(AXES), 1 << bit), 2)


def gather_bits(shard, order):
    held, block = [], shard
    for bit in reversed(order):
        other = swap_with(block, bit)
        at = sum(1 for b in held if b > bit)
        upper = side(bit) == 1
        first = jnp.where(upper, other, block)
        second = jnp.where(upper, block, other)
        block = jnp.stack([first, second], at)
        held.append(bit)
    return block.reshape((-1,) + shard.shape)


def scatter_bits(parts, order, kind):
    bits = len(order)
    shape = parts.shape[1:]
    block = parts.reshape((2,) * bits + shape)
    held = list(range(bits - 1, -1, -1))
    for bit in order:
        at = held.index(bit)
        mine = side(bit)
        keep = lax.dynamic_index_in_dim(block, mine, at, keepdims=False)
        give = lax.dynamic_index_in_dim(block, 1 - mine, at, keepdims=False)
        got = swap_with(give, bit)
        block = keep.astype(jnp.float32) + got.astype(jnp.float32)
        held.remove(bit)
        if held:
            block = block.astype(kind)
    return block


def sum_all(block):
    for bit in range(lax.axis_size(AXES).bit_length() - 1):
        block = block + swap_with(block, bit)
    return block


def prefix(decay, state, axis, reverse):
    peers, place = (lax.axis_size(axis), lax.axis_index(axis))
    states = lax.all_gather(state.astype(jnp.bfloat16), axis)
    factors = lax.all_gather(decay.astype(jnp.bfloat16), axis).astype(jnp.float32)
    total = jnp.zeros_like(state)
    for k in range(peers):
        at = peers - 1 - k if reverse else k
        reached = at > place if reverse else at < place
        stepped = total * factors[at][:, None, None] + states[at].astype(jnp.float32)
        total = jnp.where(reached, stepped, total)
    return total


def rms_scale(values, gain):
    return values * lax.rsqrt(jnp.mean(values * values, axis=-1, keepdims=True) + EPSILON) * gain


def gated_norm(values, gate_in, gain):
    return rms_scale(values * jax.nn.silu(gate_in), gain)


def taps_sum(extended, taps, first, step, row_count):
    total = None
    for k in range(CONV):
        start = first + step * k
        term = taps[k][None, :] * extended[start : start + row_count]
        total = term if total is None else total + term
    return total


def rates(step_raw, step_bias, decay_log):
    step_size = jax.nn.softplus(step_raw + step_bias)
    return (-step_size * jnp.exp(decay_log), step_size)


def decays(scores, decay_rate, step_size):
    cumulative = jnp.cumsum(decay_rate, axis=1)
    block_total = cumulative[:, -1]
    block_width = decay_rate.shape[1]
    causal = jnp.arange(block_width)[:, None] >= jnp.arange(block_width)[None, :]
    cum_heads = jnp.swapaxes(cumulative, 1, 2)
    difference = cum_heads[:, :, :, None] - cum_heads[:, :, None, :]
    kernel = jnp.where(causal, jnp.exp(jnp.where(causal, difference, 0.0)), 0.0)
    mixing = scores[:, None] * kernel * jnp.swapaxes(step_size, 1, 2)[:, :, None, :]
    weight = jnp.exp(block_total[:, None, :] - cumulative) * step_size
    growth = jnp.exp(cumulative)
    return (mixing, weight, growth, block_total)


def advance(state_now, inputs_pair):
    shrink_log, fresh_state = inputs_pair
    return (jnp.exp(shrink_log)[:, None, None] * state_now + fresh_state, state_now)


def retreat(later_grad, inputs_pair):
    shrink_log, direct = inputs_pair
    return (direct + jnp.exp(shrink_log)[:, None, None] * later_grad, later_grad)


def contract_rows(left_side, right_side):
    return lax.dot_general(
        left_side, right_side, (((0,), (0,)), ((), ())), preferred_element_type=jnp.float32
    )


def contract_cols(left_side, right_side):
    return lax.dot_general(
        left_side, right_side, (((1,), (1,)), ((), ())), preferred_element_type=jnp.float32
    )


def forward_layer(hidden, params, head_params):
    gain_in, gate_w, conv_w, taps, offset, gain_out, out_w = params
    step_bias, decay_log, skip_scale = head_params
    row_count = hidden.shape[0]
    groups = row_count // GROUP
    scaled_in, pull_norm = jax.vjp(rms_scale, hidden, gain_in)
    normed = scaled_in.astype(jnp.bfloat16)
    conv_step = jnp.dot(normed, conv_w, preferred_element_type=jnp.float32)
    gate_in = jnp.dot(normed, gate_w, preferred_element_type=jnp.float32)
    conv_in = conv_step[:, :CHANNELS]
    step_raw = conv_step[:, CHANNELS : CHANNELS + HEADS]
    edge_rows = passed_along(conv_in[row_count - (CONV - 1) :], "ctx", 1)
    extended = jnp.concatenate([edge_rows, conv_in], 0)
    before_act = offset + taps_sum(extended, taps, 0, 1, row_count)
    act_gate = jax.nn.sigmoid(before_act)
    act = before_act * act_gate
    values = act[:, :INNER].astype(jnp.bfloat16).reshape(groups, GROUP, HEADS, HDIM)
    write_keys = act[:, INNER : INNER + STATE].astype(jnp.bfloat16).reshape(groups, GROUP, STATE)
    read_keys = act[:, INNER + STATE :].astype(jnp.bfloat16).reshape(groups, GROUP, STATE)
    (decay_rate, step_size), pull_rate = jax.vjp(rates, step_raw, step_bias, decay_log)
    scores = jnp.einsum("ctn,csn->cts", read_keys, write_keys, preferred_element_type=jnp.float32)
    (mixing, weight, growth, block_total), pull_decay = jax.vjp(
        decays,
        scores,
        decay_rate.reshape(groups, GROUP, HEADS),
        step_size.reshape(groups, GROUP, HEADS),
    )
    mixing_low = mixing.astype(jnp.bfloat16)
    diagonal = jnp.einsum("chts,cshp->cthp", mixing_low, values, preferred_element_type=jnp.float32)
    scaled = (values.astype(jnp.float32) * weight[..., None]).astype(jnp.bfloat16)
    update = jnp.einsum("cshp,csn->chpn", scaled, write_keys, preferred_element_type=jnp.float32)
    empty_state = jnp.zeros((HEADS, HDIM, STATE), jnp.float32)
    local_end, _ = lax.scan(advance, empty_state, (block_total, update))
    device_decay = jnp.exp(jnp.sum(block_total, axis=0))
    incoming = prefix(device_decay, local_end, "ctx", False)
    _, states = lax.scan(advance, incoming, (block_total, update))
    held_low = states.astype(jnp.bfloat16)
    carried = jnp.einsum("ctn,chpn->cthp", read_keys, held_low, preferred_element_type=jnp.float32)
    mixed_out = (
        diagonal + growth[..., None] * carried + skip_scale[:, None] * values.astype(jnp.float32)
    )
    mixed_out = mixed_out.reshape(row_count, INNER)
    normed_float, pull_gate = jax.vjp(gated_norm, mixed_out, gate_in, gain_out)
    normed_out = normed_float.astype(jnp.bfloat16)
    branch = jnp.dot(normed_out, out_w, preferred_element_type=jnp.float32)
    kept_values = (
        normed,
        pull_norm,
        extended,
        before_act,
        act_gate,
        pull_rate,
        pull_decay,
        values,
        write_keys,
        read_keys,
        mixing_low,
        scaled,
        states,
        held_low,
        carried,
        growth,
        weight,
        block_total,
        device_decay,
        pull_gate,
        normed_out,
    )
    return (hidden + branch, kept_values)


def backward_layer(grad_hidden, params, head_params, kept_values):
    gain_in, gate_w, conv_w, taps, offset, gain_out, out_w = params
    skip_scale = head_params[2]
    (
        normed,
        pull_norm,
        extended,
        before_act,
        act_gate,
        pull_rate,
        pull_decay,
        values,
        write_keys,
        read_keys,
        mixing_low,
        scaled,
        states,
        held_low,
        carried,
        growth,
        weight,
        block_total,
        device_decay,
        pull_gate,
        normed_out,
    ) = kept_values
    row_count = grad_hidden.shape[0]
    groups = row_count // GROUP
    grad_branch = grad_hidden.astype(jnp.bfloat16)
    out_grad = contract_rows(normed_out, grad_branch)
    grad_normed = contract_cols(grad_branch, out_w)
    grad_mixed, grad_gate, gain_out_grad = pull_gate(grad_normed)
    grad_y = grad_mixed.astype(jnp.bfloat16).reshape(groups, GROUP, HEADS, HDIM)
    grad_float = grad_y.astype(jnp.float32)
    grad_mixing = jnp.einsum("cthp,cshp->chts", grad_y, values, preferred_element_type=jnp.float32)
    grad_values = jnp.einsum(
        "chts,cthp->cshp", mixing_low, grad_y, preferred_element_type=jnp.float32
    )
    grad_values = grad_values + skip_scale[:, None] * grad_float
    skip_grad = jnp.sum(grad_float * values, axis=(0, 1, 3))
    grad_growth = jnp.sum(grad_float * carried, axis=-1)
    grad_carried = (growth[..., None] * grad_float).astype(jnp.bfloat16)
    grad_read = jnp.einsum(
        "cthp,chpn->ctn", grad_carried, held_low, preferred_element_type=jnp.float32
    )
    grad_held = jnp.einsum(
        "cthp,ctn->chpn", grad_carried, read_keys, preferred_element_type=jnp.float32
    )
    empty_state = jnp.zeros((HEADS, HDIM, STATE), jnp.float32)
    local_start, _ = lax.scan(retreat, empty_state, (block_total, grad_held), reverse=True)
    outgoing = prefix(device_decay, local_start, "ctx", True)
    _, after_grad = lax.scan(retreat, outgoing, (block_total, grad_held), reverse=True)
    grad_total = jnp.exp(block_total) * jnp.sum(after_grad * states, axis=(2, 3))
    grad_update = after_grad.astype(jnp.bfloat16)
    grad_scaled = jnp.einsum(
        "chpn,csn->cshp", grad_update, write_keys, preferred_element_type=jnp.float32
    )
    grad_write = jnp.einsum(
        "chpn,cshp->csn", grad_update, scaled, preferred_element_type=jnp.float32
    )
    grad_values = grad_values + grad_scaled * weight[..., None]
    grad_weight = jnp.sum(grad_scaled * values, axis=-1)
    grad_scores, grad_rate, grad_step = pull_decay(
        (grad_mixing, grad_weight, grad_growth, grad_total)
    )
    grad_scores_low = grad_scores.astype(jnp.bfloat16)
    grad_read = grad_read + jnp.einsum(
        "cts,csn->ctn", grad_scores_low, write_keys, preferred_element_type=jnp.float32
    )
    grad_write = grad_write + jnp.einsum(
        "cts,ctn->csn", grad_scores_low, read_keys, preferred_element_type=jnp.float32
    )
    grad_raw, bias_grad, decay_grad = pull_rate(
        (grad_rate.reshape(row_count, HEADS), grad_step.reshape(row_count, HEADS))
    )
    grad_act = jnp.concatenate(
        [
            grad_values.reshape(row_count, INNER),
            grad_write.reshape(row_count, STATE),
            grad_read.reshape(row_count, STATE),
        ],
        1,
    )
    grad_before = grad_act * (act_gate * (1.0 + before_act * (1.0 - act_gate)))
    next_rows = passed_along(grad_before[: CONV - 1], "ctx", -1)
    grad_conv_in = taps_sum(
        jnp.concatenate([grad_before, next_rows], 0), taps, CONV - 1, -1, row_count
    )
    tap_grads = [
        jnp.sum(grad_before * extended[k : k + row_count], axis=0) for k in range(CONV)
    ]
    offset_grad = jnp.sum(grad_before, axis=0)
    grad_gate_low = grad_gate.astype(jnp.bfloat16)
    grad_conv_low = jnp.concatenate(
        [grad_conv_in, jnp.pad(grad_raw, ((0, 0), (0, EXTRA - HEADS)))], 1
    ).astype(jnp.bfloat16)
    gate_w_grad = contract_rows(normed, grad_gate_low)
    conv_w_grad = contract_rows(normed, grad_conv_low)
    grad_normed_in = contract_cols(grad_gate_low, gate_w) + contract_cols(grad_conv_low, conv_w)
    grad_input, gain_in_grad = pull_norm(grad_normed_in)
    weight_grads = (gate_w_grad, conv_w_grad, out_grad)
    small_grads = (gain_in_grad, tap_grads, offset_grad, gain_out_grad)
    return (grad_hidden + grad_input, weight_grads, small_grads, (bias_grad, decay_grad, skip_grad))


def on_device(
    inputs,
    cotangent,
    norm_gain,
    proj_weight,
    step_weight,
    conv_weight,
    conv_bias,
    gate_gain,
    out_weight,
    step_bias,
    decay_log,
    skip_scale,
):
    count = lax.axis_size(AXES)
    orders = bit_orders()
    d_own, ch_own, in_own = (norm_gain.shape[1], conv_bias.shape[1], gate_gain.shape[1])
    smalls = jnp.concatenate(
        [
            norm_gain.reshape(-1),
            gate_gain.reshape(-1),
            conv_bias.reshape(-1),
            conv_weight.reshape(-1),
        ]
    )
    smalls = gather_bits(smalls, orders[0]).astype(jnp.float32)
    cut = 0
    rows = []
    for own, number in ((d_own, LAYERS), (in_own, LAYERS), (ch_own, LAYERS), (ch_own, LAYERS * CONV)):
        rows.append([smalls[:, cut + i * own : cut + (i + 1) * own].reshape(-1) for i in range(number)])
        cut += own * number
    gain_rows, gate_rows, bias_rows, tap_rows = rows

    def gather_layer(shards):
        gate_part, conv_part, out_part = shards
        return (
            gather_bits(gate_part, orders[0]).reshape(-1, INNER),
            gather_bits(conv_part, orders[1]).reshape(-1, CHANNELS + EXTRA),
            gather_bits(out_part, orders[2]).reshape(INNER, -1),
        )

    shards = []
    for layer in range(LAYERS):
        shards.append(
            (
                proj_weight[layer, :, :INNER],
                jnp.concatenate(
                    [
                        proj_weight[layer, :, INNER:],
                        jnp.pad(step_weight[layer], ((0, 0), (0, EXTRA - HEADS))),
                    ],
                    1,
                ),
                out_weight[layer],
            )
        )
    gathered = []
    for layer in range(LAYERS):
        if layer > 0:
            shards[layer], _ = lax.optimization_barrier((shards[layer], gathered[layer - 1]))
        gathered.append(gather_layer(shards[layer]))

    hidden = inputs.astype(jnp.float32)
    saved_list, params_list = ([], [])
    for layer in range(LAYERS):
        gate_w, conv_w, out_w = gathered[layer]
        params = (
            gain_rows[layer],
            gate_w,
            conv_w,
            tap_rows[layer * CONV : (layer + 1) * CONV],
            bias_rows[layer],
            gate_rows[layer],
            out_w,
        )
        params_list.append(params)
        head_params = (step_bias[layer], decay_log[layer], skip_scale[layer])
        hidden, kept_values = forward_layer(hidden, params, head_params)
        saved_list.append(kept_values)
    outputs = hidden.astype(jnp.bfloat16)
    grad_hidden = cotangent.astype(jnp.float32)
    summed = [None] * LAYERS
    small_list = [None] * LAYERS
    head_list = [None] * LAYERS
    for layer in reversed(range(LAYERS)):
        head_params = (step_bias[layer], decay_log[layer], skip_scale[layer])
        grad_hidden, weight_grads, small_grads, head_grads = backward_layer(
            grad_hidden, params_list[layer], head_params, saved_list[layer]
        )
        summed[layer] = tuple(
            scatter_bits(
                grad.astype(jnp.bfloat16).reshape(count, -1, grad.shape[1]), order, jnp.bfloat16
            )
            for grad, order in zip(weight_grads, orders)
        )
        gain_in_grad, tap_grads, offset_grad, gain_out_grad = small_grads
        small_list[layer] = jnp.concatenate(
            [row.reshape(count, -1) for row in (gain_in_grad, gain_out_grad, offset_grad, *tap_grads)], 1
        )
        head_list[layer] = jnp.stack(head_grads)
    small_sums = scatter_bits(jnp.stack(small_list, 1), orders[0], jnp.float32)
    head_sums = sum_all(jnp.stack(head_list, 1))
    edge = d_own + in_own
    proj_all = jnp.stack(
        [jnp.concatenate([gate, conv[:, :CHANNELS]], 1) for gate, conv, _ in summed]
    )
    rate_all = jnp.stack([conv[:, CHANNELS : CHANNELS + HEADS] for _, conv, _ in summed])
    out_all = jnp.stack([out for _, _, out in summed])
    return (
        outputs,
        grad_hidden,
        small_sums[:, :d_own],
        proj_all,
        rate_all,
        small_sums[:, edge + ch_own :].reshape(LAYERS, CONV, ch_own),
        small_sums[:, edge : edge + ch_own],
        small_sums[:, d_own:edge],
        out_all,
        head_sums[0],
        head_sums[1],
        head_sums[2],
    )


def solution(mesh):
    in_specs = (
        P(("dp", "ctx"), None),
        P(("dp", "ctx"), None),
        P(None, ("dp", "ctx")),
        P(None, ("dp", "ctx"), None),
        P(None, ("dp", "ctx"), None),
        P(None, None, ("dp", "ctx")),
        P(None, ("dp", "ctx")),
        P(None, ("dp", "ctx")),
        P(None, ("dp", "ctx"), None),
        P(),
        P(),
        P(),
    )
    out_specs = (
        P(("dp", "ctx"), None),
        P(("dp", "ctx"), None),
        P(None, ("dp", "ctx")),
        P(None, ("dp", "ctx"), None),
        P(None, ("dp", "ctx"), None),
        P(None, None, ("dp", "ctx")),
        P(None, ("dp", "ctx")),
        P(None, ("dp", "ctx")),
        P(None, ("dp", "ctx"), None),
        P(),
        P(),
        P(),
    )
    return jax.shard_map(
        on_device, mesh=mesh, in_specs=in_specs, out_specs=out_specs, check_vma=False
    )
```

time: 1430 us -> 668 us (0.47)
  waiting for transfers between devices: 804 us -> 179 us
  blocking collectives: 207 us -> 10.1 us
  starting transfers between devices: 8.66 us -> 77.2 us
  local copies, waits for them, and re-layouts: 179 us -> 151 us
  other arithmetic: 102 us -> 128 us
  matrix products: 110 us -> 92.8 us
    reduce_scatter x4 -> x0, waiting for transfers between devices: 512 us -> none  [on_device(): lax.psum_scatter(flat_grads, ('dp', 'ctx'), scatter_dimension=0, tiled=True)]
    unnamed x16 -> x4, waiting for transfers between devices: 291 us -> 0.07 us
    all_gather x7 -> x2, blocking collectives: 207 us -> 10.1 us  [prefix(): lax.all_gather(decay.astype(jnp.bfloat16), axis).astype(jnp.float32)]
    ppermute x0 -> x75, waiting for transfers between devices: none -> 179 us  [swap_with(): return lax.ppermute(block, AXES, [(i, i ^ 1 << bit) for i in range(count)])]
    slice x5 -> x19, local copies, waits for them, and re-layouts: 78.6 us -> 9.9 us  [the longest x2 2.81 us: forward_layer(): conv_in = conv_step[:, :CHANNELS]]
    ppermute x0 -> x75, starting transfers between devices: none -> 68.1 us  [swap_with(): return lax.ppermute(block, AXES, [(i, i ^ 1 << bit) for i in range(count)])]
    another operation x23 -> x97, other arithmetic: 23.4 us -> 60.3 us
    select_n x16 -> x1, other arithmetic: 19.1 us -> 0.01 us  [gather_bits(): first = jnp.where(upper, other, block)]
  transfers between devices with their start and end apart: 17 -> 83, of which waited for: 9 -> 40; matrix products, arithmetic and copies ran while one was open for 15% -> 39% of each run, Pallas kernels for 0% -> 0%
where the time goes in v1:
time: 668 us; the launch traced here: 656 us
  waiting for transfers between devices  179 us (27%)
  local copies, waits for them, and re-layouts  151 us (23%)
  other arithmetic  128 us (19%)
  matrix products  92.8 us (14%)
  starting transfers between devices  77.2 us (12%)
  between operations  17.8 us (3%)
  blocking collectives  10.1 us (2%)
    ppermute x75, waiting for transfers between devices, swap_with(): return lax.ppermute(block, AXES, [(i, i ^ 1 << bit) for i in range(count)])  179 us
    ppermute x75, starting transfers between devices, swap_with(): return lax.ppermute(block, AXES, [(i, i ^ 1 << bit) for i in range(count)])  68.1 us
    another operation x16, other arithmetic  30.6 us
    another operation x68, other arithmetic, gather_bits(): block = jnp.stack([first, second], at)  24.8 us
    unnamed x425, local copies, waits for them, and re-layouts  17.9 us
    dot_general x6, matrix products, contract_rows(): lax.dot_general(left_side, right_side, (((0,), (0,)), ((), ())), preferre...  14.2 us
    concatenate x16, local copies, waits for them, and re-layouts, on_device(): jnp.concatenate([row.reshape(count, -1) for row in (gain_in_grad, gain_ou...  13.6 us
  transfers between devices with their start and end apart: 83, of which 40 were waited for; matrix products, arithmetic and copies ran while one was open for 39% of the time, Pallas kernels for 0%

profile of v1, /device:TPU:0, one launch (start us, length us, event | category | flops | bytes accessed | tf_op | source)
XLA Modules:
  0.0 655.7 jit_solution(4128256595357442720)
XLA Ops:
  49.7 11.9 %collective-permute-done.6 = bf16[2,24,1920]{2,1,0:T(8,128)(2,1)S(1)} collective-permute-done((bf16[2,24,1920]{2,1,0:T(8,128)(2,1)S(1)}, bf16[2,24,1920]{2,1,0:T(8,128)(2,1)S(1)}, u32[]{:S(2)}, u32[]{:S(2)}) %collective-permute-start.6) | collective-permute-done | bytes 184352 | tf_op jit(solution)/shard_map/ppermute | solution.py:31
  61.8 4.8 collective-permute-done.18
  68.5 6.0 collective-permute-done.7
  75.2 11.8 %collective-permute-done.19 = bf16[2,2,2,48,768]{4,3,2,1,0:T(8,128)(2,1)S(1)} collective-permute-done((bf16[2,2,2,48,768]{4,3,2,1,0:T(8,128)(2,1)S(1)}, bf16[2,2,2,48,768]{4,3,2,1,0:T(8,128)(2,1)S(1)}, u32[]{:S(2)}, u32[]{:S(2)}) %collective-permute-start.19) | collective-permute-done | bytes 589856 | tf_op jit(solution)/shard_map/ppermute | solution.py:31
  112.9 5.0 all-gather
  161.3 13.4 %collective-permute-done.22 = bf16[2,24,1920]{2,1,0:T(8,128)(2,1)S(1)} collective-permute-done((bf16[2,24,1920]{2,1,0:T(8,128)(2,1)S(1)}, bf16[2,24,1920]{2,1,0:T(8,128)(2,1)S(1)}, u32[]{:S(2)}, u32[]{:S(2)}) %collective-permute-start.22) | collective-permute-done | bytes 184352 | tf_op jit(solution)/shard_map/ppermute | solution.py:31
  174.8 5.7 collective-permute-done.34
  181.1 7.3 %collective-permute-done.23 = bf16[2,2,24,1920]{3,2,1,0:T(8,128)(2,1)S(1)} collective-permute-done((bf16[2,2,24,1920]{3,2,1,0:T(8,128)(2,1)S(1)}, bf16[2,2,24,1920]{3,2,1,0:T(8,128)(2,1)S(1)}, u32[]{:S(2)}, u32[]{:S(2)}) %collective-permute-start.23) | collective-permute-done | bytes 368672 | tf_op jit(solution)/shard_map/ppermute | solution.py:31
  190.1 10.8 %collective-permute-done.35 = bf16[2,2,2,48,768]{4,3,1,2,0:T(8,128)(2,1)S(1)} collective-permute-done((bf16[2,2,2,48,768]{4,3,1,2,0:T(8,128)(2,1)S(1)}, bf16[2,2,2,48,768]{4,3,1,2,0:T(8,128)(2,1)S(1)}, u32[]{:S(2)}, u32[]{:S(2)}) %collective-permute-start.35) | collective-permute-done | bytes 589856 | tf_op jit(solution)/shard_map/ppermute | solution.py:31
  256.0 5.8 multiply_convert_fusion.6
  274.9 5.1 all-gather.2
  341.3 5.8 fusion.5
  368.7 12.5 %collective-permute-done.71 = bf16[2,2,48,768]{3,2,0,1:T(8,128)(2,1)S(1)} collective-permute-done((bf16[2,2,48,768]{3,2,0,1:T(8,128)(2,1)S(1)}, bf16[2,2,48,768]{3,2,0,1:T(8,128)(2,1)S(1)}, u32[]{:S(2)}, u32[]{:S(2)}) %collective-permute-start.71) | collective-permute-done | bytes 294944 | tf_op jit(solution)/shard_map/ppermute | solution.py:31
  381.6 5.5 collective-permute-done.72
  417.9 4.9 fusion.49
  425.8 5.6 multiply_reduce_fusion.5
  477.0 6.0 fusion.7
  496.0 9.5 %collective-permute-done.45 = bf16[2,2,2,24,1536]{4,3,0,1,2:T(8,128)(2,1)S(1)} collective-permute-done((bf16[2,2,2,24,1536]{4,3,0,1,2:T(8,128)(2,1)S(1)}, bf16[2,2,2,24,1536]{4,3,0,1,2:T(8,128)(2,1)S(1)}, u32[]{:S(2)}, u32[]{:S(2)}) %collective-permute-start.45) | collective-permute-done | bytes 589856 | tf_op jit(solution)/shard_map/ppermute | solution.py:31
  508.0 11.0 %collective-permute-done.46 = bf16[2,2,24,1536]{3,2,0,1:T(8,128)(2,1)S(1)} collective-permute-done((bf16[2,2,24,1536]{3,2,0,1:T(8,128)(2,1)S(1)}, bf16[2,2,24,1536]{3,2,0,1:T(8,128)(2,1)S(1)}, u32[]{:S(2)}, u32[]{:S(2)}) %collective-permute-start.46) | collective-permute-done | bytes 294944 | tf_op jit(solution)/shard_map/ppermute | solution.py:31
  543.3 5.1 fusion.48
  557.8 6.5 multiply_reduce_fusion.9
  618.3 6.0 collective-permute-done.50
  625.6 8.5 %collective-permute-done.51 = bf16[2,2,24,1920]{3,2,1,0:T(8,128)(2,1)S(1)} collective-permute-done((bf16[2,2,24,1920]{3,2,1,0:T(8,128)(2,1)S(1)}, bf16[2,2,24,1920]{3,2,1,0:T(8,128)(2,1)S(1)}, u32[]{:S(2)}, u32[]{:S(2)}) %collective-permute-start.51) | collective-permute-done | bytes 368672 | tf_op jit(solution)/shard_map/ppermute | solution.py:31
  636.3 6.1 collective-permute-done.52
  (972 shorter events, 457.4 us)
Async XLA Ops:
  7.2 204.3 %all-gather.11.cloned.1.call-start = ((), (), s32[]{:S(2)}) async-start(), calls=%async_computation | async-start | bytes 1966080 | tf_op jit(solution)/shard_map/all_gather | solution.py:86
  8.2 31.2 %collective-permute-start.16 = (bf16[48,768]{1,0:T(8,128)(2,1)S(1)}, bf16[48,768]{1,0:T(8,128)(2,1)S(1)}, u32[]{:S(2)}, u32[]{:S(2)}) collective-permute-start(bf16[48,768]{1,0:T(8,128)(2,1)S(1)} %get-tuple-element.269), channel_id=1, source_target_pairs={{0,4},{1,5},{2,6},{3,7},{4,0},{5,1},{6,2},{7,3},{8,12},{9,13},{10,... | collective-permute-start | bytes 221192 | tf_op jit(solution)/shard_map/ppermute | solution.py:31
  12.9 29.7 %collective-permute-start.5 = (bf16[24,1920]{1,0:T(8,128)(2,1)S(1)}, bf16[24,1920]{1,0:T(8,128)(2,1)S(1)}, u32[]{:S(2)}, u32[]{:S(2)}) collective-permute-start(bf16[24,1920]{1,0:T(8,128)(2,1)S(1)} %fusion.141), channel_id=1, source_target_pairs={{0,2},{1,3},{2,0},{3,1},{4,6},{5,7},{6,4},{7,5},{8,10},{9,11},{10,... | collective-permute-start | bytes 276488 | tf_op jit(solution)/shard_map/ppermute | solution.py:31
  21.1 19.0 %collective-permute-start.11 = (bf16[24,1536]{1,0:T(8,128)(2,1)S(1)}, bf16[24,1536]{1,0:T(8,128)(2,1)S(1)}, u32[]{:S(2)}, u32[]{:S(2)}) collective-permute-start(bf16[24,1536]{1,0:T(8,128)(2,1)S(1)} %get-tuple-element.249), channel_id=1, source_target_pairs={{0,16},{1,17},{2,18},{3,19},{4,20},{5,21},{6,22},{7,23},{8,24},{9,... | collective-permute-start | bytes 221192 | tf_op jit(solution)/shard_map/ppermute | solution.py:31
  42.7 18.9 %collective-permute-start.6 = (bf16[2,24,1920]{2,1,0:T(8,128)(2,1)S(1)}, bf16[2,24,1920]{2,1,0:T(8,128)(2,1)S(1)}, u32[]{:S(2)}, u32[]{:S(2)}) collective-permute-start(bf16[2,24,1920]{2,1,0:T(8,128)(2,1)S(1)} %pad_maximum_fusion.30), channel_id=1, source_target_pairs={{0,16},{1,17},{2,18},{3,19},{4,20},{5,21},{6,22},{7,23},{8,24},{9,... | collective-permute-start | bytes 552968 | tf_op jit(solution)/shard_map/ppermute | solution.py:31
  45.5 21.0 %collective-permute-start.18 = (bf16[2,2,48,768]{3,2,1,0:T(8,128)(2,1)S(1)}, bf16[2,2,48,768]{3,2,1,0:T(8,128)(2,1)S(1)}, u32[]{:S(2)}, u32[]{:S(2)}) collective-permute-start(bf16[2,2,48,768]{3,2,1,0:T(8,128)(2,1)S(1)} %pad_maximum_fusion.26), channel_id=1, source_target_pairs={{0,16},{1,17},{2,18},{3,19},{4,20},{5,21},{6,22},{7,23},{8,24},{9,... | collective-permute-start | bytes 884744 | tf_op jit(solution)/shard_map/ppermute | solution.py:31
  66.7 20.3 %collective-permute-start.19 = (bf16[2,2,2,48,768]{4,3,2,1,0:T(8,128)(2,1)S(1)}, bf16[2,2,2,48,768]{4,3,2,1,0:T(8,128)(2,1)S(1)}, u32[]{:S(2)}, u32[]{:S(2)}) collective-permute-start(bf16[2,2,2,48,768]{4,3,2,1,0:T(8,128)(2,1)S(1)} %pad_maximum_fusion.20), channel_id=1, source_target_pairs={{0,8},{1,9},{2,10},{3,11},{4,12},{5,13},{6,14},{7,15},{8,0},{9,1},... | collective-permute-start | bytes 1769480 | tf_op jit(solution)/shard_map/ppermute | solution.py:31
  66.9 21.4 %collective-permute-start.14 = (bf16[2,2,2,24,1536]{4,3,2,1,0:T(8,128)(2,1)S(1)}, bf16[2,2,2,24,1536]{4,3,2,1,0:T(8,128)(2,1)S(1)}, u32[]{:S(2)}, u32[]{:S(2)}) collective-permute-start(bf16[2,2,2,24,1536]{4,3,2,1,0:T(8,128)(2,1)S(1)} %pad_maximum_fusion.19), channel_id=1, source_target_pairs={{0,2},{1,3},{2,0},{3,1},{4,6},{5,7},{6,4},{7,5},{8,10},{9,11},{10,... | collective-permute-start | bytes 1769480 | tf_op jit(solution)/shard_map/ppermute | solution.py:31
  74.6 18.4 %collective-permute-start.8 = (bf16[2,2,2,24,1920]{4,3,2,1,0:T(8,128)(2,1)S(1)}, bf16[2,2,2,24,1920]{4,3,2,1,0:T(8,128)(2,1)S(1)}, u32[]{:S(2)}, u32[]{:S(2)}) collective-permute-start(bf16[2,2,2,24,1920]{4,3,2,1,0:T(8,128)(2,1)S(1)} %pad_maximum_fusion.16), channel_id=1, source_target_pairs={{0,4},{1,5},{2,6},{3,7},{4,0},{5,1},{6,2},{7,3},{8,12},{9,13},{10,... | collective-permute-start | bytes 2211848 | tf_op jit(solution)/shard_map/ppermute | solution.py:31
  121.4 34.0 %collective-permute-start.21 = (bf16[24,1920]{1,0:T(8,128)(2,1)S(1)}, bf16[24,1920]{1,0:T(8,128)(2,1)}, u32[]{:S(2)}, u32[]{:S(2)}) collective-permute-start(bf16[24,1920]{1,0:T(8,128)(2,1)S(1)} %fusion.142), channel_id=1, source_target_pairs={{0,2},{1,3},{2,0},{3,1},{4,6},{5,7},{6,4},{7,5},{8,10},{9,11},{10,... | collective-permute-start | bytes 276488 | tf_op jit(solution)/shard_map/ppermute | solution.py:31
  123.0 28.9 %collective-permute-start.27 = (bf16[24,1536]{1,0:T(8,128)(2,1)S(1)}, bf16[24,1536]{1,0:T(8,128)(2,1)}, u32[]{:S(2)}, u32[]{:S(2)}) collective-permute-start(bf16[24,1536]{1,0:T(8,128)(2,1)S(1)} %get-tuple-element.116), channel_id=1, source_target_pairs={{0,16},{1,17},{2,18},{3,19},{4,20},{5,21},{6,22},{7,23},{8,24},{9,... | collective-permute-start | bytes 221192 | tf_op jit(solution)/shard_map/ppermute | solution.py:31
  129.9 20.5 %collective-permute-start.32 = (bf16[48,768]{1,0:T(8,128)(2,1)S(1)}, bf16[48,768]{1,0:T(8,128)(2,1)}, u32[]{:S(2)}, u32[]{:S(2)}) collective-permute-start(bf16[48,768]{1,0:T(8,128)(2,1)S(1)} %get-tuple-element.117), channel_id=1, source_target_pairs={{0,4},{1,5},{2,6},{3,7},{4,0},{5,1},{6,2},{7,3},{8,12},{9,13},{10,... | collective-permute-start | bytes 221192 | tf_op jit(solution)/shard_map/ppermute | solution.py:31
  147.9 151.5 %all-gather.13.cloned.1.call-start = ((), (), s32[]{:S(2)}) async-start(), calls=%async_computation.1 | async-start | bytes 1966080 | tf_op jit(solution)/shard_map/all_gather | solution.py:86
  156.8 23.7 %collective-permute-start.34 = (bf16[2,2,48,768]{3,2,0,1:T(8,128)(2,1)S(1)}, bf16[2,2,48,768]{3,2,0,1:T(8,128)(2,1)S(1)}, u32[]{:S(2)}, u32[]{:S(2)}) collective-permute-start(bf16[2,2,48,768]{3,2,0,1:T(8,128)(2,1)S(1)} %pad_maximum_fusion.28), channel_id=1, source_target_pairs={{0,16},{1,17},{2,18},{3,19},{4,20},{5,21},{6,22},{7,23},{8,24},{9,... | collective-permute-start | bytes 884744 | tf_op jit(solution)/shard_map/ppermute | solution.py:31
  159.7 21.0 %collective-permute-start.29 = (bf16[2,2,24,1536]{3,2,0,1:T(8,128)(2,1)S(1)}, bf16[2,2,24,1536]{3,2,0,1:T(8,128)(2,1)S(1)}, u32[]{:S(2)}, u32[]{:S(2)}) collective-permute-start(bf16[2,2,24,1536]{3,2,0,1:T(8,128)(2,1)S(1)} %pad_maximum_fusion.27), channel_id=1, source_target_pairs={{0,4},{1,5},{2,6},{3,7},{4,0},{5,1},{6,2},{7,3},{8,12},{9,13},{10,... | collective-permute-start | bytes 884744 | tf_op jit(solution)/shard_map/ppermute | solution.py:31
  180.6 20.3 %collective-permute-start.35 = (bf16[2,2,2,48,768]{4,3,1,2,0:T(8,128)(2,1)S(1)}, bf16[2,2,2,48,768]{4,3,1,2,0:T(8,128)(2,1)S(1)}, u32[]{:S(2)}, u32[]{:S(2)}) collective-permute-start(bf16[2,2,2,48,768]{4,3,1,2,0:T(8,128)(2,1)S(1)} %pad_maximum_fusion.22), channel_id=1, source_target_pairs={{0,8},{1,9},{2,10},{3,11},{4,12},{5,13},{6,14},{7,15},{8,0},{9,1},... | collective-permute-start | bytes 1769480 | tf_op jit(solution)/shard_map/ppermute | solution.py:31
  180.8 20.4 %collective-permute-start.30 = (bf16[2,2,2,24,1536]{4,3,0,1,2:T(8,128)(2,1)S(1)}, bf16[2,2,2,24,1536]{4,3,0,1,2:T(8,128)(2,1)S(1)}, u32[]{:S(2)}, u32[]{:S(2)}) collective-permute-start(bf16[2,2,2,24,1536]{4,3,0,1,2:T(8,128)(2,1)S(1)} %pad_maximum_fusion.21), channel_id=1, source_target_pairs={{0,2},{1,3},{2,0},{3,1},{4,6},{5,7},{6,4},{7,5},{8,10},{9,11},{10,... | collective-permute-start | bytes 1769480 | tf_op jit(solution)/shard_map/ppermute | solution.py:31
  202.6 66.0 %collective-permute-start.31 = (bf16[2,2,2,2,24,1536]{5,4,0,1,2,3:T(8,128)(2,1)}, bf16[2,2,2,2,24,1536]{5,4,0,1,2,3:T(8,128)(2,1)}, u32[]{:S(2)}, u32[]{:S(2)}) collective-permute-start(bf16[2,2,2,2,24,1536]{5,4,0,1,2,3:T(8,128)(2,1)} %pad_maximum_fusion.14), channel_id=1, source_target_pairs={{0,1},{1,0},{2,3},{3,2},{4,5},{5,4},{6,7},{7,6},{8,9},{9,8},{10,11... | collective-permute-start | bytes 3538952 | tf_op jit(solution)/shard_map/ppermute | solution.py:31
  230.1 25.9 %collective-permute-start.26 = (f32[3,1792]{1,0:T(4,128)}, f32[3,1792]{1,0:T(4,128)}, u32[]{:S(2)}, u32[]{:S(2)}) collective-permute-start(f32[3,1792]{1,0:T(4,128)} %slice.474), channel_id=1, source_target_pairs={{0,1},{1,2},{2,3},{4,5},{5,6},{6,7},{8,9},{9,10},{10,11},{12,13},{... | collective-permute-start | bytes 64520 | tf_op jit(solution)/shard_map/ppermute | solution.py:23
  268.5 126.5 %all-gather.15.cloned.1.call-start = ((), (), s32[]{:S(2)}) async-start(), calls=%async_computation.2 | async-start | bytes 1966080 | tf_op jit(solution)/shard_map/all_gather | solution.py:86
  333.5 200.9 %all-gather.17.cloned.1.call-start = ((), (), s32[]{:S(2)}) async-start(), calls=%async_computation.3 | async-start | bytes 1966080 | tf_op jit(solution)/shard_map/all_gather | solution.py:86
  466.5 26.0 %collective-permute-start.59 = (bf16[2,2,2,2,24,1920]{5,4,3,0,1,2:T(8,128)(2,1)}, bf16[2,2,2,2,24,1920]{5,4,3,0,1,2:T(8,128)(2,1)}, u32[]{:S(2)}, u32[]{:S(2)}) collective-permute-start(bf16[2,2,2,2,24,1920]{5,4,3,0,1,2:T(8,128)(2,1)} %bitcast.985), channel_id=1, source_target_pairs={{0,1},{1,0},{2,3},{3,2},{4,5},{5,4},{6,7},{7,6},{8,9},{9,8},{10,11... | collective-permute-start | bytes 4423688 | tf_op jit(solution)/shard_map/ppermute | solution.py:31
  494.4 36.4 %collective-permute-start.60 = (bf16[2,2,2,24,1920]{4,3,2,0,1:T(8,128)(2,1)S(1)}, bf16[2,2,2,24,1920]{4,3,2,0,1:T(8,128)(2,1)S(1)}, u32[]{:S(2)}, u32[]{:S(2)}) collective-permute-start(bf16[2,2,2,24,1920]{4,3,2,0,1:T(8,128)(2,1)S(1)} %dynamic-slice_bitcast_fusion), channel_id=1, source_target_pairs={{0,4},{1,5},{2,6},{3,7},{4,0},{5,1},{6,2},{7,3},{8,12},{9,13},{10,... | collective-permute-start | bytes 2211848 | tf_op jit(solution)/shard_map/ppermute | solution.py:31
  532.7 72.1 %collective-permute-start.61 = (bf16[2,2,24,1920]{3,2,1,0:T(8,128)(2,1)}, bf16[2,2,24,1920]{3,2,1,0:T(8,128)(2,1)}, u32[]{:S(2)}, u32[]{:S(2)}) collective-permute-start(bf16[2,2,24,1920]{3,2,1,0:T(8,128)(2,1)} %dynamic-slice_bitcast_fusion.6), channel_id=1, source_target_pairs={{0,8},{1,9},{2,10},{3,11},{4,12},{5,13},{6,14},{7,15},{8,0},{9,1},... | collective-permute-start | bytes 1105928 | tf_op jit(solution)/shard_map/ppermute | solution.py:31
  (269 other events, 1980.0 us)
Sparse Core Ops, SparseCore 0:
  148.0 18.9 all-gather.10
  268.6 17.7 all-gather.12
  333.7 17.7 all-gather.14
  463.3 18.5 all-gather.16

commit v2 on v1

--- a/solution.py
+++ b/solution.py
@@ -1,6 +1,8 @@
 import jax
 import jax.numpy as jnp
 from jax import lax
+from jax.experimental import pallas as pl
+from jax.experimental.pallas import tpu as pltpu
 from jax.sharding import PartitionSpec as P
 
 HEADS = 24
@@ -116,28 +118,168 @@
     return (-step_size * jnp.exp(decay_log), step_size)
 
 
-def decays(scores, decay_rate, step_size):
-    cumulative = jnp.cumsum(decay_rate, axis=1)
-    block_total = cumulative[:, -1]
-    block_width = decay_rate.shape[1]
-    causal = jnp.arange(block_width)[:, None] >= jnp.arange(block_width)[None, :]
-    cum_heads = jnp.swapaxes(cumulative, 1, 2)
-    difference = cum_heads[:, :, :, None] - cum_heads[:, :, None, :]
-    kernel = jnp.where(causal, jnp.exp(jnp.where(causal, difference, 0.0)), 0.0)
-    mixing = scores[:, None] * kernel * jnp.swapaxes(step_size, 1, 2)[:, :, None, :]
-    weight = jnp.exp(block_total[:, None, :] - cumulative) * step_size
-    growth = jnp.exp(cumulative)
-    return (mixing, weight, growth, block_total)
-
-
-def advance(state_now, inputs_pair):
-    shrink_log, fresh_state = inputs_pair
-    return (jnp.exp(shrink_log)[:, None, None] * state_now + fresh_state, state_now)
-
-
-def retreat(later_grad, inputs_pair):
-    shrink_log, direct = inputs_pair
-    return (direct + jnp.exp(shrink_log)[:, None, None] * later_grad, later_grad)
+def mm(left, right, dims, exact=False):
+    return lax.dot_general(
+        left,
+        right,
+        ((dims[:1], dims[1:]), ((), ())),
+        precision=lax.Precision.HIGHEST if exact else None,
+        preferred_element_type=jnp.float32,
+    )
+
+
+PAIR = 2 * HDIM
+PAIRS = HEADS // 2
+
+
+def left_half(rows):
+    return lax.broadcasted_iota(jnp.int32, (rows, PAIR), 1) < HDIM
+
+
+def pair_of(ref, j, half):
+    return jnp.where(half, ref[:, 2 * j : 2 * j + 1], ref[:, 2 * j + 1 : 2 * j + 2])
+
+
+def head_sum(j):
+    lane = lax.broadcasted_iota(jnp.int32, (PAIR, 128), 0)
+    head = lax.broadcasted_iota(jnp.int32, (PAIR, 128), 1)
+    return (head == 2 * j + jnp.where(lane < HDIM, 0, 1)).astype(jnp.float32)
+
+
+def decay_kernel(cum, cum_t, h, causal):
+    difference = cum[:, h : h + 1] - cum_t[h : h + 1, :]
+    return jnp.exp(jnp.where(causal, difference, -jnp.inf))
+
+
+def causal_mask(rows):
+    return lax.broadcasted_iota(jnp.int32, (rows, rows), 0) >= lax.broadcasted_iota(
+        jnp.int32, (rows, rows), 1
+    )
+
+
+def mix_forward(
+    values, write, read, cum, cum_t, step_t, state, gate, skip, gain, normed, mixed, inverse, kept
+):
+    rows = values.shape[0]
+    half, causal = (left_half(rows), causal_mask(rows))
+    scores = mm(read[...], write[...], (1, 1))
+    squares = jnp.zeros((rows, PAIR), jnp.float32)
+    for j in range(PAIRS):
+        at = slice(j * PAIR, (j + 1) * PAIR)
+        pair = values[:, at]
+        parts = []
+        for h in (2 * j, 2 * j + 1):
+            mixing = scores * decay_kernel(cum, cum_t, h, causal) * step_t[h : h + 1, :]
+            parts.append(mm(mixing.astype(jnp.bfloat16), pair, (1, 0)))
+        carried = mm(read[...], state[at, :].astype(jnp.bfloat16), (1, 1))
+        out = (
+            jnp.where(half, parts[0], parts[1])
+            + jnp.exp(pair_of(cum, j, half)) * carried
+            + skip[:, at] * pair.astype(jnp.float32)
+        )
+        mixed[:, at] = out
+        gated = out * jax.nn.silu(gate[:, at])
+        kept[:, at] = gated
+        squares += gated * gated
+    scale = lax.rsqrt(jnp.sum(squares, axis=1, keepdims=True) / INNER + EPSILON)
+    inverse[...] = jnp.broadcast_to(scale, (rows, PAIR))
+    for j in range(PAIRS):
+        at = slice(j * PAIR, (j + 1) * PAIR)
+        normed[:, at] = (kept[:, at] * scale * gain[:, at]).astype(jnp.bfloat16)
+
+
+def gate_backward(
+    grad, values, read, cum, state, gate, gain, mixed, inverse,
+    grad_y, grad_gate, gain_grad, skip_grad, growth_grad, read_grad, held_grad,
+):
+    rows = values.shape[0]
+    half = left_half(rows)
+    scale = inverse[...]
+    total = jnp.zeros((rows, PAIR), jnp.float32)
+    for j in range(PAIRS):
+        at = slice(j * PAIR, (j + 1) * PAIR)
+        unit = mixed[:, at] * jax.nn.silu(gate[:, at]) * scale
+        product = grad[:, at] * unit
+        gain_grad[:, at] = jnp.sum(product, axis=0, keepdims=True)
+        total += product * gain[:, at]
+    mean = jnp.sum(total, axis=1, keepdims=True) / INNER
+    growths = jnp.zeros((rows, 128), jnp.float32)
+    reads = jnp.zeros((rows, STATE), jnp.float32)
+    for j in range(PAIRS):
+        at = slice(j * PAIR, (j + 1) * PAIR)
+        gate_now, mixed_now = (gate[:, at], mixed[:, at])
+        sig = jax.nn.sigmoid(gate_now)
+        silu = gate_now * sig
+        direct = scale * (grad[:, at] * gain[:, at] - mixed_now * silu * scale * mean)
+        low = (direct * silu).astype(jnp.bfloat16)
+        grad_y[:, at] = low
+        slope = sig * (1.0 + gate_now * (1.0 - sig))
+        grad_gate[:, at] = (direct * mixed_now * slope).astype(jnp.bfloat16)
+        wide = low.astype(jnp.float32)
+        held = state[at, :].astype(jnp.bfloat16)
+        carried = mm(read[...], held, (1, 1))
+        growths += mm(wide * carried, head_sum(j), (1, 0), True)
+        skip_grad[:, at] = jnp.sum(wide * values[:, at].astype(jnp.float32), axis=0, keepdims=True)
+        grad_carried = (jnp.exp(pair_of(cum, j, half)) * wide).astype(jnp.bfloat16)
+        reads += mm(grad_carried, held, (1, 0))
+        held_grad[at, :] = mm(grad_carried, read[...], (0, 0))
+    growth_grad[...] = growths
+    read_grad[...] = reads
+
+
+def mix_backward(
+    grad_y, values, write, read, cum, cum_t, step_t, weight, after, skip, read_part,
+    grad_values, grad_write, grad_read, row_grad, column_grad, weight_grad,
+):
+    rows = values.shape[0]
+    half, causal = (left_half(rows), causal_mask(rows))
+    scores = mm(read[...], write[...], (1, 1))
+    score_grad = jnp.zeros((rows, rows), jnp.float32)
+    writes = jnp.zeros((rows, STATE), jnp.float32)
+    weights = jnp.zeros((rows, 128), jnp.float32)
+    for j in range(PAIRS):
+        at = slice(j * PAIR, (j + 1) * PAIR)
+        pair, upper = (values[:, at], grad_y[:, at])
+        wide, upper_wide = (pair.astype(jnp.float32), upper.astype(jnp.float32))
+        update = after[at, :].astype(jnp.bfloat16)
+        scaled_grad = mm(write[...], update, (1, 1))
+        spread = pair_of(weight, j, half)
+        writes += mm((wide * spread).astype(jnp.bfloat16), update, (1, 0))
+        parts = []
+        for i in range(2):
+            h = 2 * j + i
+            own = jnp.where(half if i == 0 else jnp.logical_not(half), upper_wide, 0.0)
+            mixing_grad = mm(own.astype(jnp.bfloat16), pair, (1, 1))
+            factor = decay_kernel(cum, cum_t, h, causal)
+            stepped = factor * step_t[h : h + 1, :]
+            mixing = scores * stepped
+            score_grad += mixing_grad * stepped
+            row_grad[:, h : h + 1] = jnp.sum(mixing_grad * mixing, axis=1, keepdims=True)
+            column_grad[h : h + 1, :] = jnp.sum(
+                mixing_grad * (scores * factor), axis=0, keepdims=True
+            )
+            parts.append(mm(mixing.astype(jnp.bfloat16), upper, (0, 0)))
+        grad_values[:, at] = (
+            jnp.where(half, parts[0], parts[1]) + skip[:, at] * upper_wide + scaled_grad * spread
+        )
+        weights += mm(scaled_grad * wide, head_sum(j), (1, 0), True)
+    low = score_grad.astype(jnp.bfloat16)
+    grad_read[...] = read_part[...] + mm(low, write[...], (1, 0))
+    grad_write[...] = writes + mm(low, read[...], (0, 0))
+    weight_grad[...] = weights
+
+
+def on_core(body, outs, scratch=()):
+    return pl.pallas_call(
+        body,
+        out_shape=[jax.ShapeDtypeStruct(shape, kind) for shape, kind in outs],
+        scratch_shapes=list(scratch),
+        compiler_params=pltpu.CompilerParams(vmem_limit_bytes=28 * 1024 * 1024),
+    )
+
+
+def lower_ones(rows):
+    return causal_mask(rows).astype(jnp.float32)
 
 
 def contract_rows(left_side, right_side):
@@ -156,7 +298,7 @@
     gain_in, gate_w, conv_w, taps, offset, gain_out, out_w = params
     step_bias, decay_log, skip_scale = head_params
     row_count = hidden.shape[0]
-    groups = row_count // GROUP
+    assert row_count == GROUP
     scaled_in, pull_norm = jax.vjp(rms_scale, hidden, gain_in)
     normed = scaled_in.astype(jnp.bfloat16)
     conv_step = jnp.dot(normed, conv_w, preferred_element_type=jnp.float32)
@@ -168,34 +310,31 @@
     before_act = offset + taps_sum(extended, taps, 0, 1, row_count)
     act_gate = jax.nn.sigmoid(before_act)
     act = before_act * act_gate
-    values = act[:, :INNER].astype(jnp.bfloat16).reshape(groups, GROUP, HEADS, HDIM)
-    write_keys = act[:, INNER : INNER + STATE].astype(jnp.bfloat16).reshape(groups, GROUP, STATE)
-    read_keys = act[:, INNER + STATE :].astype(jnp.bfloat16).reshape(groups, GROUP, STATE)
+    act_low = act.astype(jnp.bfloat16)
+    values = act_low[:, :INNER]
+    write_keys = act_low[:, INNER : INNER + STATE]
+    read_keys = act_low[:, INNER + STATE :]
     (decay_rate, step_size), pull_rate = jax.vjp(rates, step_raw, step_bias, decay_log)
-    scores = jnp.einsum("ctn,csn->cts", read_keys, write_keys, preferred_element_type=jnp.float32)
-    (mixing, weight, growth, block_total), pull_decay = jax.vjp(
-        decays,
-        scores,
-        decay_rate.reshape(groups, GROUP, HEADS),
-        step_size.reshape(groups, GROUP, HEADS),
-    )
-    mixing_low = mixing.astype(jnp.bfloat16)
-    diagonal = jnp.einsum("chts,cshp->cthp", mixing_low, values, preferred_element_type=jnp.float32)
-    scaled = (values.astype(jnp.float32) * weight[..., None]).astype(jnp.bfloat16)
-    update = jnp.einsum("cshp,csn->chpn", scaled, write_keys, preferred_element_type=jnp.float32)
-    empty_state = jnp.zeros((HEADS, HDIM, STATE), jnp.float32)
-    local_end, _ = lax.scan(advance, empty_state, (block_total, update))
-    device_decay = jnp.exp(jnp.sum(block_total, axis=0))
-    incoming = prefix(device_decay, local_end, "ctx", False)
-    _, states = lax.scan(advance, incoming, (block_total, update))
-    held_low = states.astype(jnp.bfloat16)
-    carried = jnp.einsum("ctn,chpn->cthp", read_keys, held_low, preferred_element_type=jnp.float32)
-    mixed_out = (
-        diagonal + growth[..., None] * carried + skip_scale[:, None] * values.astype(jnp.float32)
-    )
-    mixed_out = mixed_out.reshape(row_count, INNER)
-    normed_float, pull_gate = jax.vjp(gated_norm, mixed_out, gate_in, gain_out)
-    normed_out = normed_float.astype(jnp.bfloat16)
+    cumulative = mm(lower_ones(row_count), decay_rate, (1, 0), True)
+    block_total = cumulative[-1]
+    shrink = jnp.exp(block_total[None, :] - cumulative)
+    weight = shrink * step_size
+    cum_t, step_t = (cumulative.T, step_size.T)
+    spread = jnp.broadcast_to(weight[:, :, None], (row_count, HEADS, HDIM)).reshape(row_count, INNER)
+    scaled = (values.astype(jnp.float32) * spread).astype(jnp.bfloat16)
+    update = contract_rows(scaled, write_keys).reshape(HEADS, HDIM, STATE)
+    device_decay = jnp.exp(block_total)
+    incoming = prefix(device_decay, update, "ctx", False).reshape(INNER, STATE)
+    skip_row = jnp.repeat(skip_scale, HDIM)[None, :]
+    wide = (row_count, INNER)
+    normed_out, mixed_out, inverse = on_core(
+        mix_forward,
+        [(wide, jnp.bfloat16), (wide, jnp.float32), ((row_count, PAIR), jnp.float32)],
+        [pltpu.VMEM(wide, jnp.float32)],
+    )(
+        values, write_keys, read_keys, cumulative, cum_t, step_t, incoming, gate_in,
+        skip_row, gain_out[None, :],
+    )
     branch = jnp.dot(normed_out, out_w, preferred_element_type=jnp.float32)
     kept_values = (
         normed,
@@ -204,20 +343,21 @@
         before_act,
         act_gate,
         pull_rate,
-        pull_decay,
         values,
         write_keys,
         read_keys,
-        mixing_low,
-        scaled,
-        states,
-        held_low,
-        carried,
-        growth,
+        cumulative,
+        cum_t,
+        step_t,
+        step_size,
+        shrink,
         weight,
-        block_total,
         device_decay,
-        pull_gate,
+        incoming,
+        skip_row,
+        gate_in,
+        mixed_out,
+        inverse,
         normed_out,
     )
     return (hidden + branch, kept_values)
@@ -233,79 +373,63 @@
         before_act,
         act_gate,
         pull_rate,
-        pull_decay,
         values,
         write_keys,
         read_keys,
-        mixing_low,
-        scaled,
-        states,
-        held_low,
-        carried,
-        growth,
+        cumulative,
+        cum_t,
+        step_t,
+        step_size,
+        shrink,
         weight,
-        block_total,
         device_decay,
-        pull_gate,
+        incoming,
+        skip_row,
+        gate_in,
+        mixed_out,
+        inverse,
         normed_out,
     ) = kept_values
     row_count = grad_hidden.shape[0]
-    groups = row_count // GROUP
     grad_branch = grad_hidden.astype(jnp.bfloat16)
     out_grad = contract_rows(normed_out, grad_branch)
     grad_normed = contract_cols(grad_branch, out_w)
-    grad_mixed, grad_gate, gain_out_grad = pull_gate(grad_normed)
-    grad_y = grad_mixed.astype(jnp.bfloat16).reshape(groups, GROUP, HEADS, HDIM)
-    grad_float = grad_y.astype(jnp.float32)
-    grad_mixing = jnp.einsum("cthp,cshp->chts", grad_y, values, preferred_element_type=jnp.float32)
-    grad_values = jnp.einsum(
-        "chts,cthp->cshp", mixing_low, grad_y, preferred_element_type=jnp.float32
-    )
-    grad_values = grad_values + skip_scale[:, None] * grad_float
-    skip_grad = jnp.sum(grad_float * values, axis=(0, 1, 3))
-    grad_growth = jnp.sum(grad_float * carried, axis=-1)
-    grad_carried = (growth[..., None] * grad_float).astype(jnp.bfloat16)
-    grad_read = jnp.einsum(
-        "cthp,chpn->ctn", grad_carried, held_low, preferred_element_type=jnp.float32
-    )
-    grad_held = jnp.einsum(
-        "cthp,ctn->chpn", grad_carried, read_keys, preferred_element_type=jnp.float32
-    )
-    empty_state = jnp.zeros((HEADS, HDIM, STATE), jnp.float32)
-    local_start, _ = lax.scan(retreat, empty_state, (block_total, grad_held), reverse=True)
-    outgoing = prefix(device_decay, local_start, "ctx", True)
-    _, after_grad = lax.scan(retreat, outgoing, (block_total, grad_held), reverse=True)
-    grad_total = jnp.exp(block_total) * jnp.sum(after_grad * states, axis=(2, 3))
-    grad_update = after_grad.astype(jnp.bfloat16)
-    grad_scaled = jnp.einsum(
-        "chpn,csn->cshp", grad_update, write_keys, preferred_element_type=jnp.float32
-    )
-    grad_write = jnp.einsum(
-        "chpn,cshp->csn", grad_update, scaled, preferred_element_type=jnp.float32
-    )
-    grad_values = grad_values + grad_scaled * weight[..., None]
-    grad_weight = jnp.sum(grad_scaled * values, axis=-1)
-    grad_scores, grad_rate, grad_step = pull_decay(
-        (grad_mixing, grad_weight, grad_growth, grad_total)
-    )
-    grad_scores_low = grad_scores.astype(jnp.bfloat16)
-    grad_read = grad_read + jnp.einsum(
-        "cts,csn->ctn", grad_scores_low, write_keys, preferred_element_type=jnp.float32
-    )
-    grad_write = grad_write + jnp.einsum(
-        "cts,ctn->csn", grad_scores_low, read_keys, preferred_element_type=jnp.float32
-    )
-    grad_raw, bias_grad, decay_grad = pull_rate(
-        (grad_rate.reshape(row_count, HEADS), grad_step.reshape(row_count, HEADS))
-    )
-    grad_act = jnp.concatenate(
+    wide, keys = ((row_count, INNER), (row_count, STATE))
+    row = (1, INNER)
+    grad_y, grad_gate_low, gain_out_grad, skip_grad, growth_grad, read_part, grad_held = on_core(
+        gate_backward,
         [
-            grad_values.reshape(row_count, INNER),
-            grad_write.reshape(row_count, STATE),
-            grad_read.reshape(row_count, STATE),
+            (wide, jnp.bfloat16), (wide, jnp.bfloat16), (row, jnp.float32), (row, jnp.float32),
+            ((row_count, 128), jnp.float32), (keys, jnp.float32), ((INNER, STATE), jnp.float32),
         ],
-        1,
-    )
+    )(grad_normed, values, read_keys, cumulative, incoming, gate_in, gain_out[None, :], mixed_out, inverse)
+    skip_grad = jnp.sum(skip_grad.reshape(HEADS, HDIM), axis=1)
+    outgoing = prefix(device_decay, grad_held.reshape(HEADS, HDIM, STATE), "ctx", True)
+    grad_total = device_decay * jnp.sum(
+        outgoing * incoming.reshape(HEADS, HDIM, STATE), axis=(1, 2)
+    )
+    grad_values, grad_write, grad_read, row_grad, column_grad, weight_grad = on_core(
+        mix_backward,
+        [
+            (wide, jnp.float32), (keys, jnp.float32), (keys, jnp.float32),
+            ((row_count, HEADS), jnp.float32), ((HEADS, row_count), jnp.float32),
+            ((row_count, 128), jnp.float32),
+        ],
+    )(
+        grad_y, values, write_keys, read_keys, cumulative, cum_t, step_t, weight,
+        outgoing.reshape(INNER, STATE), skip_row, read_part,
+    )
+    growth_grad, weight_grad = (growth_grad[:, :HEADS], weight_grad[:, :HEADS])
+    column_grad = column_grad.T
+    through_weight = weight * weight_grad
+    grad_cum = (
+        row_grad - step_size * column_grad + jnp.exp(cumulative) * growth_grad - through_weight
+    )
+    grad_total = grad_total + jnp.sum(through_weight, axis=0)
+    grad_rate = mm(lower_ones(row_count), grad_cum, (0, 0), True) + grad_total
+    grad_step = column_grad + shrink * weight_grad
+    grad_raw, bias_grad, decay_grad = pull_rate((grad_rate, grad_step))
+    grad_act = jnp.concatenate([grad_values, grad_write, grad_read], 1)
     grad_before = grad_act * (act_gate * (1.0 + before_act * (1.0 - act_gate)))
     next_rows = passed_along(grad_before[: CONV - 1], "ctx", -1)
     grad_conv_in = taps_sum(
@@ -315,7 +439,6 @@
         jnp.sum(grad_before * extended[k : k + row_count], axis=0) for k in range(CONV)
     ]
     offset_grad = jnp.sum(grad_before, axis=0)
-    grad_gate_low = grad_gate.astype(jnp.bfloat16)
     grad_conv_low = jnp.concatenate(
         [grad_conv_in, jnp.pad(grad_raw, ((0, 0), (0, EXTRA - HEADS)))], 1
     ).astype(jnp.bfloat16)
@@ -425,7 +548,7 @@
         )
         gain_in_grad, tap_grads, offset_grad, gain_out_grad = small_grads
         small_list[layer] = jnp.concatenate(
-            [row.reshape(count, -1) for row in (gain_in_grad, gain_out_grad, offset_grad, *tap_grads)], 1
+            [line.reshape(count, -1) for line in (gain_in_grad, gain_out_grad, offset_grad, *tap_grads)], 1
         )
         head_list[layer] = jnp.stack(head_grads)
     small_sums = scatter_bits(jnp.stack(small_list, 1), orders[0], jnp.float32)

time: 668 us -> 566 us (0.85)
  matrix products: 92.8 us -> 27.7 us
  local copies, waits for them, and re-layouts: 151 us -> 96 us
  Pallas kernels: 0 us -> 32.4 us
  other arithmetic: 128 us -> 106 us
  waiting for transfers between devices: 179 us -> 194 us
    dot_general x24 -> x4, matrix products: 56.6 us -> 4.93 us  [mm(): lax.dot_general(left, right, ((dims[:1], dims[1:]), ((), ())), precision=...]
    pallas_call x0 -> x6, Pallas kernels: none -> 32.4 us  [the longest x2 18.3 us: backward_layer(): on_core(mix_backward, [(wide, jnp.float32), (keys, jnp.float32), (keys, j...]
    another operation x16 -> x2, other arithmetic: 30.6 us -> 8.8 us
    convert_element_type x10 -> x0, local copies, waits for them, and re-layouts: 19.5 us -> none  [the longest x2 4.7 us: forward_layer(): (values.astype(jnp.float32) * weight[..., None]).astype(jnp.bfloat16)]
    mul x9 -> x2, local copies, waits for them, and re-layouts: 18.6 us -> 0.74 us  [forward_layer(): weight = shrink * step_size]
    convert_element_type x4 -> x10, other arithmetic: 5.01 us -> 19.9 us  [the longest x2 10.9 us: forward_layer(): act_low = act.astype(jnp.bfloat16)]
    ppermute x75, waiting for transfers between devices: 179 us -> 193 us  [swap_with(): return lax.ppermute(block, AXES, [(i, i ^ 1 << bit) for i in range(count)])]
    mul x2 -> x26, local copies, waits for them, and re-layouts: 1.87 us -> 16.4 us  [prefix(): total * factors[at][:, None, None] + states[at].astype(jnp.float32)]
  transfers between devices with their start and end apart: 83 -> 83, of which waited for: 40 -> 41; matrix products, arithmetic and copies ran while one was open for 39% -> 33% of each run, Pallas kernels for 0% -> 5%
where the time goes in v2:
time: 566 us; the launch traced here: 556 us
  waiting for transfers between devices  194 us (34%)
  other arithmetic  106 us (19%)
  local copies, waits for them, and re-layouts  96 us (17%)
  starting transfers between devices  72.1 us (13%)
  Pallas kernels  32.4 us (6%)
  matrix products  27.7 us (5%)
  between operations  18 us (3%)
  blocking collectives  10.1 us (2%)
    ppermute x75, waiting for transfers between devices, swap_with(): return lax.ppermute(block, AXES, [(i, i ^ 1 << bit) for i in range(count)])  193 us
    ppermute x75, starting transfers between devices, swap_with(): return lax.ppermute(block, AXES, [(i, i ^ 1 << bit) for i in range(count)])  63.2 us
    unnamed x415, local copies, waits for them, and re-layouts  19.1 us
    pallas_call x2, Pallas kernels, backward_layer(): on_core(mix_backward, [(wide, jnp.float32), (keys, jnp.float32), (keys, j...  18.3 us
    another operation x68, other arithmetic, gather_bits(): block = jnp.stack([first, second], at)  17.3 us
    mul x26, local copies, waits for them, and re-layouts, prefix(): total * factors[at][:, None, None] + states[at].astype(jnp.float32)  16.4 us
    select_n x4, other arithmetic, prefix(): total = jnp.where(reached, stepped, total)  13.9 us
    convert_element_type x24, other arithmetic, scatter_bits(): block = block.astype(kind)  13.5 us
  transfers between devices with their start and end apart: 83, of which 41 were waited for; matrix products, arithmetic and copies ran while one was open for 33% of the time, Pallas kernels for 5%

profile of v2, /device:TPU:0, one launch (start us, length us, event | category | flops | bytes accessed | tf_op | source)
XLA Modules:
  0.0 556.0 jit_solution(9471211105392195343)
XLA Ops:
  51.8 11.0 %collective-permute-done.6 = bf16[2,24,1920]{2,1,0:T(8,128)(2,1)S(1)} collective-permute-done((bf16[2,24,1920]{2,1,0:T(8,128)(2,1)S(1)}, bf16[2,24,1920]{2,1,0:T(8,128)(2,1)S(1)}, u32[]{:S(2)}, u32[]{:S(2)}) %collective-permute-start.6) | collective-permute-done | bytes 184352 | tf_op jit(solution)/shard_map/ppermute | solution.py:33
  68.0 7.7 %collective-permute-done.7 = bf16[2,2,24,1920]{3,2,1,0:T(8,128)(2,1)S(1)} collective-permute-done((bf16[2,2,24,1920]{3,2,1,0:T(8,128)(2,1)S(1)}, bf16[2,2,24,1920]{3,2,1,0:T(8,128)(2,1)S(1)}, u32[]{:S(2)}, u32[]{:S(2)}) %collective-permute-start.7) | collective-permute-done | bytes 368672 | tf_op jit(solution)/shard_map/ppermute | solution.py:33
  76.5 11.8 %collective-permute-done.19 = bf16[2,2,2,48,768]{4,3,2,1,0:T(8,128)(2,1)S(1)} collective-permute-done((bf16[2,2,2,48,768]{4,3,2,1,0:T(8,128)(2,1)S(1)}, bf16[2,2,2,48,768]{4,3,2,1,0:T(8,128)(2,1)S(1)}, u32[]{:S(2)}, u32[]{:S(2)}) %collective-permute-start.19) | collective-permute-done | bytes 589856 | tf_op jit(solution)/shard_map/ppermute | solution.py:33
  89.3 5.0 collective-permute-done.8
  107.7 5.0 all-gather
  124.6 5.1 multiply_convert_fusion.1
  144.3 10.3 %collective-permute-done.22 = bf16[2,24,1920]{2,1,0:T(8,128)(2,1)S(1)} collective-permute-done((bf16[2,24,1920]{2,1,0:T(8,128)(2,1)S(1)}, bf16[2,24,1920]{2,1,0:T(8,128)(2,1)S(1)}, u32[]{:S(2)}, u32[]{:S(2)}) %collective-permute-start.22) | collective-permute-done | bytes 184352 | tf_op jit(solution)/shard_map/ppermute | solution.py:33
  160.4 7.7 %collective-permute-done.23 = bf16[2,2,24,1920]{3,2,1,0:T(8,128)(2,1)S(1)} collective-permute-done((bf16[2,2,24,1920]{3,2,1,0:T(8,128)(2,1)S(1)}, bf16[2,2,24,1920]{3,2,1,0:T(8,128)(2,1)S(1)}, u32[]{:S(2)}, u32[]{:S(2)}) %collective-permute-start.23) | collective-permute-done | bytes 368672 | tf_op jit(solution)/shard_map/ppermute | solution.py:33
  171.2 9.5 %collective-permute-done.35 = bf16[2,2,2,48,768]{4,3,1,2,0:T(8,128)(2,1)S(1)} collective-permute-done((bf16[2,2,2,48,768]{4,3,1,2,0:T(8,128)(2,1)S(1)}, bf16[2,2,2,48,768]{4,3,1,2,0:T(8,128)(2,1)S(1)}, u32[]{:S(2)}, u32[]{:S(2)}) %collective-permute-start.35) | collective-permute-done | bytes 589856 | tf_op jit(solution)/shard_map/ppermute | solution.py:33
  214.2 5.8 %multiply_convert_fusion = (bf16[256,1792]{1,0:T(8,128)(2,1)S(1)}, f32[256,1792]{1,0:T(8,128)}) fusion(f32[256,1792]{1,0:T(8,128)} %slice.434, f32[1792]{0:T(1024)} %mul.752, f32[3,1792]{1,0:T(4,128)} %collective-permute-done.26, f32[1792]{0:T(1024)} %mul.749, f32[1792]{0:T(1024)} %mul.746, f32[1792]{0:T(1024)} %mul.737, f32[1792]{0:T(1024)} %add.597), kind=kLoop, calls=%fused_computation.74 | loop fusion | flops 7340032 | bytes 4644864 | tf_op jit(solution)/shard_map/convert_element_type | solution.py:313
  230.9 5.0 all-gather.1
  255.7 9.8 %fusion.75.state = f32[1536,128]{1,0:T(8,128)S(1)} fusion(f32[1,24,64,128]{3,2,1,0:T(8,128)S(1)} %get-tuple-element.153, f32[1,24,64,128]{3,2,1,0:T(8,128)S(1)} %get-tuple-element.154, f32[1,24,64,128]{3,2,1,0:T(8,128)S(1)} %get-tuple-element.155, f32[1,24,64,128]{3,2,1,0:T(8,128)S(1)} %get-tuple-element.152, f32[1536]{0:T(1024)S(1)} %copy-done.164, ...), kind=kLoop, calls=%fused_computation.200 | loop fusion | flops 2162688 | bytes 3956740 | tf_op jit(solution)/shard_map/jit(_where)/select_n | solution.py:95
  295.3 11.4 %collective-permute-done.55 = bf16[2,2,2,24,1536]{4,3,0,1,2:T(8,128)(2,1)} collective-permute-done((bf16[2,2,2,24,1536]{4,3,0,1,2:T(8,128)(2,1)S(1)}, bf16[2,2,2,24,1536]{4,3,0,1,2:T(8,128)(2,1)}, u32[]{:S(2)}, u32[]{:S(2)}) %collective-permute-start.55) | collective-permute-done | bytes 589856 | tf_op jit(solution)/shard_map/ppermute | solution.py:33
  315.1 11.0 %collective-permute-done.71 = bf16[2,2,48,768]{3,2,0,1:T(8,128)(2,1)S(1)} collective-permute-done((bf16[2,2,48,768]{3,2,0,1:T(8,128)(2,1)S(1)}, bf16[2,2,48,768]{3,2,0,1:T(8,128)(2,1)S(1)}, u32[]{:S(2)}, u32[]{:S(2)}) %collective-permute-start.71) | collective-permute-done | bytes 294944 | tf_op jit(solution)/shard_map/ppermute | solution.py:33
  342.5 9.1 %shard_map.214 = (f32[256,1536]{1,0:T(8,128)S(1)}, f32[256,128]{1,0:T(8,128)S(1)}, f32[256,128]{1,0:T(8,128)S(1)}, f32[256,24]{1,0:T(8,128)S(1)}, f32[24,256]{1,0:T(8,128)S(1)}, /*index=5*/f32[256,128]{1,0:T(8,128)S(1)}) custom-call(bf16[256,1536]{1,0:T(8,128)(2,1)S(1)} %copy-done.25, bf16[256,1536]{1,0:T(8,128)(2,1)S(1)} %copy-done.3, ...), custom_call_target="tpu_custom_call" | custom-call | tf_op jit(solution)/shard_map/pallas_call | solution.py:411
  352.9 5.1 multiply_reduce_fusion.1
  400.5 10.0 %collective-permute-done.65 = bf16[2,2,2,48,768]{4,3,1,2,0:T(8,128)(2,1)S(1)} collective-permute-done((bf16[2,2,2,48,768]{4,3,1,2,0:T(8,128)(2,1)S(1)}, bf16[2,2,2,48,768]{4,3,1,2,0:T(8,128)(2,1)S(1)}, u32[]{:S(2)}, u32[]{:S(2)}) %collective-permute-start.65) | collective-permute-done | bytes 589856 | tf_op jit(solution)/shard_map/ppermute | solution.py:33
  410.9 9.6 %collective-permute-done.45 = bf16[2,2,2,24,1536]{4,3,0,1,2:T(8,128)(2,1)S(1)} collective-permute-done((bf16[2,2,2,24,1536]{4,3,0,1,2:T(8,128)(2,1)S(1)}, bf16[2,2,2,24,1536]{4,3,0,1,2:T(8,128)(2,1)S(1)}, u32[]{:S(2)}, u32[]{:S(2)}) %collective-permute-start.45) | collective-permute-done | bytes 589856 | tf_op jit(solution)/shard_map/ppermute | solution.py:33
  421.6 5.0 collective-permute-done.66
  446.1 9.2 %shard_map.216 = (f32[256,1536]{1,0:T(8,128)S(1)}, f32[256,128]{1,0:T(8,128)S(1)}, f32[256,128]{1,0:T(8,128)S(1)}, f32[256,24]{1,0:T(8,128)S(1)}, f32[24,256]{1,0:T(8,128)S(1)}, /*index=5*/f32[256,128]{1,0:T(8,128)S(1)}) custom-call(bf16[256,1536]{1,0:T(8,128)(2,1)S(1)} %copy-done.27, bf16[256,1536]{1,0:T(8,128)(2,1)S(1)} %copy-done.1, ...), custom_call_target="tpu_custom_call" | custom-call | tf_op jit(solution)/shard_map/pallas_call | solution.py:411
  469.0 5.2 multiply_reduce_fusion.5
  515.2 9.1 %collective-permute-done.50 = bf16[2,2,2,24,1920]{4,3,2,0,1:T(8,128)(2,1)S(1)} collective-permute-done((bf16[2,2,2,24,1920]{4,3,2,0,1:T(8,128)(2,1)}, bf16[2,2,2,24,1920]{4,3,2,0,1:T(8,128)(2,1)S(1)}, u32[]{:S(2)}, u32[]{:S(2)}) %collective-permute-start.50) | collective-permute-done | bytes 737312 | tf_op jit(solution)/shard_map/ppermute | solution.py:33
  526.1 8.0 %collective-permute-done.51 = bf16[2,2,24,1920]{3,2,1,0:T(8,128)(2,1)S(1)} collective-permute-done((bf16[2,2,24,1920]{3,2,1,0:T(8,128)(2,1)S(1)}, bf16[2,2,24,1920]{3,2,1,0:T(8,128)(2,1)S(1)}, u32[]{:S(2)}, u32[]{:S(2)}) %collective-permute-start.51) | collective-permute-done | bytes 368672 | tf_op jit(solution)/shard_map/ppermute | solution.py:33
  535.6 7.1 %collective-permute-done.52 = bf16[2,24,1920]{2,1,0:T(8,128)(2,1)S(1)} collective-permute-done((bf16[2,24,1920]{2,1,0:T(8,128)(2,1)S(1)}, bf16[2,24,1920]{2,1,0:T(8,128)(2,1)S(1)}, u32[]{:S(2)}, u32[]{:S(2)}) %collective-permute-start.52) | collective-permute-done | bytes 184352 | tf_op jit(solution)/shard_map/ppermute | solution.py:33
  (921 shorter events, 344.5 us)
Async XLA Ops:
  7.2 182.0 %all-gather.7.cloned.1.call-start = ((), (), s32[]{:S(2)}) async-start(), calls=%async_computation | async-start | bytes 1966080 | tf_op jit(solution)/shard_map/all_gather | solution.py:88
  15.3 28.0 %collective-permute-start.16 = (bf16[48,768]{1,0:T(8,128)(2,1)S(1)}, bf16[48,768]{1,0:T(8,128)(2,1)S(1)}, u32[]{:S(2)}, u32[]{:S(2)}) collective-permute-start(bf16[48,768]{1,0:T(8,128)(2,1)S(1)} %get-tuple-element.217), channel_id=1, source_target_pairs={{0,4},{1,5},{2,6},{3,7},{4,0},{5,1},{6,2},{7,3},{8,12},{9,13},{10,... | collective-permute-start | bytes 221192 | tf_op jit(solution)/shard_map/ppermute | solution.py:33
  17.8 22.9 %collective-permute-start.11 = (bf16[24,1536]{1,0:T(8,128)(2,1)S(1)}, bf16[24,1536]{1,0:T(8,128)(2,1)S(1)}, u32[]{:S(2)}, u32[]{:S(2)}) collective-permute-start(bf16[24,1536]{1,0:T(8,128)(2,1)S(1)} %get-tuple-element.197), channel_id=1, source_target_pairs={{0,16},{1,17},{2,18},{3,19},{4,20},{5,21},{6,22},{7,23},{8,24},{9,... | collective-permute-start | bytes 221192 | tf_op jit(solution)/shard_map/ppermute | solution.py:33
  19.8 24.0 %collective-permute-start.5 = (bf16[24,1920]{1,0:T(8,128)(2,1)S(1)}, bf16[24,1920]{1,0:T(8,128)(2,1)S(1)}, u32[]{:S(2)}, u32[]{:S(2)}) collective-permute-start(bf16[24,1920]{1,0:T(8,128)(2,1)S(1)} %fusion.137), channel_id=1, source_target_pairs={{0,2},{1,3},{2,0},{3,1},{4,6},{5,7},{6,4},{7,5},{8,10},{9,11},{10,... | collective-permute-start | bytes 276488 | tf_op jit(solution)/shard_map/ppermute | solution.py:33
  43.9 18.8 %collective-permute-start.6 = (bf16[2,24,1920]{2,1,0:T(8,128)(2,1)S(1)}, bf16[2,24,1920]{2,1,0:T(8,128)(2,1)S(1)}, u32[]{:S(2)}, u32[]{:S(2)}) collective-permute-start(bf16[2,24,1920]{2,1,0:T(8,128)(2,1)S(1)} %pad_maximum_fusion.30), channel_id=1, source_target_pairs={{0,16},{1,17},{2,18},{3,19},{4,20},{5,21},{6,22},{7,23},{8,24},{9,... | collective-permute-start | bytes 552968 | tf_op jit(solution)/shard_map/ppermute | solution.py:33
  63.0 25.5 %collective-permute-start.14 = (bf16[2,2,2,24,1536]{4,3,2,1,0:T(8,128)(2,1)S(1)}, bf16[2,2,2,24,1536]{4,3,2,1,0:T(8,128)(2,1)S(1)}, u32[]{:S(2)}, u32[]{:S(2)}) collective-permute-start(bf16[2,2,2,24,1536]{4,3,2,1,0:T(8,128)(2,1)S(1)} %pad_maximum_fusion.19), channel_id=1, source_target_pairs={{0,2},{1,3},{2,0},{3,1},{4,6},{5,7},{6,4},{7,5},{8,10},{9,11},{10,... | collective-permute-start | bytes 1769480 | tf_op jit(solution)/shard_map/ppermute | solution.py:33
  67.9 20.3 %collective-permute-start.19 = (bf16[2,2,2,48,768]{4,3,2,1,0:T(8,128)(2,1)S(1)}, bf16[2,2,2,48,768]{4,3,2,1,0:T(8,128)(2,1)S(1)}, u32[]{:S(2)}, u32[]{:S(2)}) collective-permute-start(bf16[2,2,2,48,768]{4,3,2,1,0:T(8,128)(2,1)S(1)} %pad_maximum_fusion.20), channel_id=1, source_target_pairs={{0,8},{1,9},{2,10},{3,11},{4,12},{5,13},{6,14},{7,15},{8,0},{9,1},... | collective-permute-start | bytes 1769480 | tf_op jit(solution)/shard_map/ppermute | solution.py:33
  105.1 26.3 %collective-permute-start.27 = (bf16[24,1536]{1,0:T(8,128)(2,1)S(1)}, bf16[24,1536]{1,0:T(8,128)(2,1)}, u32[]{:S(2)}, u32[]{:S(2)}) collective-permute-start(bf16[24,1536]{1,0:T(8,128)(2,1)S(1)} %get-tuple-element.55), channel_id=1, source_target_pairs={{0,16},{1,17},{2,18},{3,19},{4,20},{5,21},{6,22},{7,23},{8,24},{9,... | collective-permute-start | bytes 221192 | tf_op jit(solution)/shard_map/ppermute | solution.py:33
  105.6 29.2 %collective-permute-start.32 = (bf16[48,768]{1,0:T(8,128)(2,1)S(1)}, bf16[48,768]{1,0:T(8,128)(2,1)}, u32[]{:S(2)}, u32[]{:S(2)}) collective-permute-start(bf16[48,768]{1,0:T(8,128)(2,1)S(1)} %get-tuple-element.57), channel_id=1, source_target_pairs={{0,4},{1,5},{2,6},{3,7},{4,0},{5,1},{6,2},{7,3},{8,12},{9,13},{10,... | collective-permute-start | bytes 221192 | tf_op jit(solution)/shard_map/ppermute | solution.py:33
  106.2 30.2 %collective-permute-start.21 = (bf16[24,1920]{1,0:T(8,128)(2,1)S(1)}, bf16[24,1920]{1,0:T(8,128)(2,1)S(1)}, u32[]{:S(2)}, u32[]{:S(2)}) collective-permute-start(bf16[24,1920]{1,0:T(8,128)(2,1)S(1)} %fusion.138), channel_id=1, source_target_pairs={{0,2},{1,3},{2,0},{3,1},{4,6},{5,7},{6,4},{7,5},{8,10},{9,11},{10,... | collective-permute-start | bytes 276488 | tf_op jit(solution)/shard_map/ppermute | solution.py:33
  131.1 122.9 %all-gather.9.cloned.1.call-start = ((), (), s32[]{:S(2)}) async-start(), calls=%async_computation.1 | async-start | bytes 1966080 | tf_op jit(solution)/shard_map/all_gather | solution.py:88
  160.3 20.3 %collective-permute-start.35 = (bf16[2,2,2,48,768]{4,3,1,2,0:T(8,128)(2,1)S(1)}, bf16[2,2,2,48,768]{4,3,1,2,0:T(8,128)(2,1)S(1)}, u32[]{:S(2)}, u32[]{:S(2)}) collective-permute-start(bf16[2,2,2,48,768]{4,3,1,2,0:T(8,128)(2,1)S(1)} %pad_maximum_fusion.22), channel_id=1, source_target_pairs={{0,8},{1,9},{2,10},{3,11},{4,12},{5,13},{6,14},{7,15},{8,0},{9,1},... | collective-permute-start | bytes 1769480 | tf_op jit(solution)/shard_map/ppermute | solution.py:33
  168.3 18.4 %collective-permute-start.24 = (bf16[2,2,2,24,1920]{4,3,2,0,1:T(8,128)(2,1)S(1)}, bf16[2,2,2,24,1920]{4,3,2,0,1:T(8,128)(2,1)S(1)}, u32[]{:S(2)}, u32[]{:S(2)}) collective-permute-start(bf16[2,2,2,24,1920]{4,3,2,0,1:T(8,128)(2,1)S(1)} %pad_maximum_fusion.17), channel_id=1, source_target_pairs={{0,4},{1,5},{2,6},{3,7},{4,0},{5,1},{6,2},{7,3},{8,12},{9,13},{10,... | collective-permute-start | bytes 2211848 | tf_op jit(solution)/shard_map/ppermute | solution.py:33
  171.2 51.1 %collective-permute-start.31 = (bf16[2,2,2,2,24,1536]{5,4,0,1,2,3:T(8,128)(2,1)}, bf16[2,2,2,2,24,1536]{5,4,0,1,2,3:T(8,128)(2,1)}, u32[]{:S(2)}, u32[]{:S(2)}) collective-permute-start(bf16[2,2,2,2,24,1536]{5,4,0,1,2,3:T(8,128)(2,1)} %pad_maximum_fusion.14), channel_id=1, source_target_pairs={{0,1},{1,0},{2,3},{3,2},{4,5},{5,4},{6,7},{7,6},{8,9},{9,8},{10,11... | collective-permute-start | bytes 3538952 | tf_op jit(solution)/shard_map/ppermute | solution.py:33
  182.0 42.2 %collective-permute-start.36 = (bf16[2,2,2,2,48,768]{5,4,2,3,0,1:T(8,128)(2,1)}, bf16[2,2,2,2,48,768]{5,4,2,3,0,1:T(8,128)(2,1)}, u32[]{:S(2)}, u32[]{:S(2)}) collective-permute-start(bf16[2,2,2,2,48,768]{5,4,2,3,0,1:T(8,128)(2,1)} %pad_maximum_fusion.15), channel_id=1, source_target_pairs={{0,1},{1,0},{2,3},{3,2},{4,5},{5,4},{6,7},{7,6},{8,9},{9,8},{10,11... | collective-permute-start | bytes 3538952 | tf_op jit(solution)/shard_map/ppermute | solution.py:33
  222.2 113.2 %all-gather.11.cloned.1.call-start = ((), (), s32[]{:S(2)}) async-start(), calls=%async_computation.2 | async-start | bytes 1966080 | tf_op jit(solution)/shard_map/all_gather | solution.py:88
  287.8 19.0 %collective-permute-start.55 = (bf16[2,2,2,24,1536]{4,3,0,1,2:T(8,128)(2,1)S(1)}, bf16[2,2,2,24,1536]{4,3,0,1,2:T(8,128)(2,1)}, u32[]{:S(2)}, u32[]{:S(2)}) collective-permute-start(bf16[2,2,2,24,1536]{4,3,0,1,2:T(8,128)(2,1)S(1)} %dynamic-slice_bitcast_fusion.4), channel_id=1, source_target_pairs={{0,2},{1,3},{2,0},{3,1},{4,6},{5,7},{6,4},{7,5},{8,10},{9,11},{10,... | collective-permute-start | bytes 1769480 | tf_op jit(solution)/shard_map/ppermute | solution.py:33
  292.0 147.6 %all-gather.13.cloned.1.call-start = ((), (), s32[]{:S(2)}) async-start(), calls=%async_computation.3 | async-start | bytes 1966080 | tf_op jit(solution)/shard_map/all_gather | solution.py:88
  333.3 54.1 %collective-permute-start.73 = (bf16[48,768]{1,0:T(8,128)(2,1)}, bf16[48,768]{1,0:T(8,128)(2,1)}, u32[]{:S(2)}, u32[]{:S(2)}) collective-permute-start(bf16[48,768]{1,0:T(8,128)(2,1)} %dynamic-slice_bitcast_fusion.20), channel_id=1, source_target_pairs={{0,4},{1,5},{2,6},{3,7},{4,0},{5,1},{6,2},{7,3},{8,12},{9,13},{10,... | collective-permute-start | bytes 221192 | tf_op jit(solution)/shard_map/ppermute | solution.py:33
  396.7 23.9 %collective-permute-start.45 = (bf16[2,2,2,24,1536]{4,3,0,1,2:T(8,128)(2,1)S(1)}, bf16[2,2,2,24,1536]{4,3,0,1,2:T(8,128)(2,1)S(1)}, u32[]{:S(2)}, u32[]{:S(2)}) collective-permute-start(bf16[2,2,2,24,1536]{4,3,0,1,2:T(8,128)(2,1)S(1)} %dynamic-slice_bitcast_fusion.5), channel_id=1, source_target_pairs={{0,2},{1,3},{2,0},{3,1},{4,6},{5,7},{6,4},{7,5},{8,10},{9,11},{10,... | collective-permute-start | bytes 1769480 | tf_op jit(solution)/shard_map/ppermute | solution.py:33
  399.6 37.7 %collective-permute-start.60 = (bf16[2,2,2,24,1920]{4,3,2,0,1:T(8,128)(2,1)S(1)}, bf16[2,2,2,24,1920]{4,3,2,0,1:T(8,128)(2,1)S(1)}, u32[]{:S(2)}, u32[]{:S(2)}) collective-permute-start(bf16[2,2,2,24,1920]{4,3,2,0,1:T(8,128)(2,1)S(1)} %dynamic-slice_bitcast_fusion), channel_id=1, source_target_pairs={{0,4},{1,5},{2,6},{3,7},{4,0},{5,1},{6,2},{7,3},{8,12},{9,13},{10,... | collective-permute-start | bytes 2211848 | tf_op jit(solution)/shard_map/ppermute | solution.py:33
  433.3 27.9 %collective-permute-start.68 = (bf16[48,768]{1,0:T(8,128)(2,1)}, bf16[48,768]{1,0:T(8,128)(2,1)}, u32[]{:S(2)}, u32[]{:S(2)}) collective-permute-start(bf16[48,768]{1,0:T(8,128)(2,1)} %dynamic-slice_bitcast_fusion.21), channel_id=1, source_target_pairs={{0,4},{1,5},{2,6},{3,7},{4,0},{5,1},{6,2},{7,3},{8,12},{9,13},{10,... | collective-permute-start | bytes 221192 | tf_op jit(solution)/shard_map/ppermute | solution.py:33
  435.8 23.1 %collective-permute-start.48 = (bf16[24,1536]{1,0:T(8,128)(2,1)}, bf16[24,1536]{1,0:T(8,128)(2,1)}, u32[]{:S(2)}, u32[]{:S(2)}) collective-permute-start(bf16[24,1536]{1,0:T(8,128)(2,1)} %dynamic-slice_bitcast_fusion.23), channel_id=1, source_target_pairs={{0,16},{1,17},{2,18},{3,19},{4,20},{5,21},{6,22},{7,23},{8,24},{9,... | collective-permute-start | bytes 221192 | tf_op jit(solution)/shard_map/ppermute | solution.py:33
  439.2 66.7 %collective-permute-start.61 = (bf16[2,2,24,1920]{3,2,1,0:T(8,128)(2,1)}, bf16[2,2,24,1920]{3,2,1,0:T(8,128)(2,1)}, u32[]{:S(2)}, u32[]{:S(2)}) collective-permute-start(bf16[2,2,24,1920]{3,2,1,0:T(8,128)(2,1)} %dynamic-slice_bitcast_fusion.6), channel_id=1, source_target_pairs={{0,8},{1,9},{2,10},{3,11},{4,12},{5,13},{6,14},{7,15},{8,0},{9,1},... | collective-permute-start | bytes 1105928 | tf_op jit(solution)/shard_map/ppermute | solution.py:33
  (266 other events, 2470.5 us)
Sparse Core Ops, SparseCore 0:
  131.2 20.3 all-gather.6
  222.3 18.1 all-gather.8
  292.1 21.0 all-gather.10
  391.9 25.8 all-gather.12

commit v3 on v2

--- a/solution.py
+++ b/solution.py
@@ -540,12 +540,7 @@
         grad_hidden, weight_grads, small_grads, head_grads = backward_layer(
             grad_hidden, params_list[layer], head_params, saved_list[layer]
         )
-        summed[layer] = tuple(
-            scatter_bits(
-                grad.astype(jnp.bfloat16).reshape(count, -1, grad.shape[1]), order, jnp.bfloat16
-            )
-            for grad, order in zip(weight_grads, orders)
-        )
+        summed[layer] = weight_grads
         gain_in_grad, tap_grads, offset_grad, gain_out_grad = small_grads
         small_list[layer] = jnp.concatenate(
             [line.reshape(count, -1) for line in (gain_in_grad, gain_out_grad, offset_grad, *tap_grads)], 1
@@ -554,11 +549,18 @@
     small_sums = scatter_bits(jnp.stack(small_list, 1), orders[0], jnp.float32)
     head_sums = sum_all(jnp.stack(head_list, 1))
     edge = d_own + in_own
-    proj_all = jnp.stack(
-        [jnp.concatenate([gate, conv[:, :CHANNELS]], 1) for gate, conv, _ in summed]
-    )
-    rate_all = jnp.stack([conv[:, CHANNELS : CHANNELS + HEADS] for _, conv, _ in summed])
-    out_all = jnp.stack([out for _, _, out in summed])
+    gate_all, conv_all, out_all = (
+        scatter_bits(
+            jnp.stack(
+                [grad.astype(jnp.bfloat16).reshape(count, -1, grad.shape[1]) for grad in grads], 1
+            ),
+            order,
+            jnp.bfloat16,
+        )
+        for grads, order in zip(zip(*summed), orders)
+    )
+    proj_all = jnp.concatenate([gate_all, conv_all[:, :, :CHANNELS]], 2)
+    rate_all = conv_all[:, :, CHANNELS : CHANNELS + HEADS]
     return (
         outputs,
         grad_hidden,

time: 566 us -> 579 us (1.023)
  waiting for transfers between devices: 194 us -> 210 us
  matrix products: 27.7 us -> 39.8 us
  starting transfers between devices: 72.1 us -> 61.7 us
  other arithmetic: 106 us -> 98.1 us
    ppermute x75 -> x60, starting transfers between devices: 63.2 us -> 52.4 us  [swap_with(): return lax.ppermute(block, AXES, [(i, i ^ 1 << bit) for i in range(count)])]
    all_gather x4, waiting for transfers between devices: 0.03 us -> 8.71 us  [prefix(): states = lax.all_gather(state.astype(jnp.bfloat16), axis)]
    dot_general x8, matrix products: 9.05 us -> 17.6 us  [contract_rows(): lax.dot_general(left_side, right_side, (((0,), (0,)), ((), ())), preferre...]
    select_n x4, other arithmetic: 13.9 us -> 5.41 us  [prefix(): total = jnp.where(reached, stepped, total)]
    ppermute x75 -> x60, waiting for transfers between devices: 193 us -> 201 us  [swap_with(): return lax.ppermute(block, AXES, [(i, i ^ 1 << bit) for i in range(count)])]
    unnamed x415 -> x408, local copies, waits for them, and re-layouts: 19.1 us -> 25.2 us
    dynamic_slice x7 -> x1, local copies, waits for them, and re-layouts: 6.03 us -> 0.01 us  [scatter_bits(): give = lax.dynamic_index_in_dim(block, 1 - mine, at, keepdims=False)]
    convert_element_type x24 -> x12, other arithmetic: 13.5 us -> 17.1 us  [scatter_bits(): block = block.astype(kind)]
  transfers between devices with their start and end apart: 83 -> 68, of which waited for: 41 -> 30; matrix products, arithmetic and copies ran while one was open for 33% -> 32% of each run, Pallas kernels for 5% -> 2%
where the time goes in v3:
time: 579 us; the launch traced here: 569 us
  waiting for transfers between devices  210 us (36%)
  local copies, waits for them, and re-layouts  100 us (17%)
  other arithmetic  98.1 us (17%)
  starting transfers between devices  61.7 us (11%)
  matrix products  39.8 us (7%)
  Pallas kernels  32.3 us (6%)
  between operations  17.4 us (3%)
  blocking collectives  10.1 us (2%)
    ppermute x60, waiting for transfers between devices, swap_with(): return lax.ppermute(block, AXES, [(i, i ^ 1 << bit) for i in range(count)])  201 us
    ppermute x60, starting transfers between devices, swap_with(): return lax.ppermute(block, AXES, [(i, i ^ 1 << bit) for i in range(count)])  52.4 us
    unnamed x408, local copies, waits for them, and re-layouts  25.2 us
    mul x26, local copies, waits for them, and re-layouts, prefix(): total * factors[at][:, None, None] + states[at].astype(jnp.float32)  19.1 us
    pallas_call x2, Pallas kernels, backward_layer(): on_core(mix_backward, [(wide, jnp.float32), (keys, jnp.float32), (keys, j...  18.2 us
    dot_general x8, matrix products, contract_rows(): lax.dot_general(left_side, right_side, (((0,), (0,)), ((), ())), preferre...  17.6 us
    another operation x68, other arithmetic, gather_bits(): block = jnp.stack([first, second], at)  17.2 us
    convert_element_type x12, other arithmetic, scatter_bits(): block = block.astype(kind)  17.1 us
  transfers between devices with their start and end apart: 68, of which 30 were waited for; matrix products, arithmetic and copies ran while one was open for 32% of the time, Pallas kernels for 2%

profile of v3, /device:TPU:0, one launch (start us, length us, event | category | flops | bytes accessed | tf_op | source)
XLA Modules:
  0.0 569.2 jit_solution(1204563426872152131)
XLA Ops:
  54.1 11.0 %collective-permute-done.6 = bf16[2,24,1920]{2,1,0:T(8,128)(2,1)S(1)} collective-permute-done((bf16[2,24,1920]{2,1,0:T(8,128)(2,1)S(1)}, bf16[2,24,1920]{2,1,0:T(8,128)(2,1)S(1)}, u32[]{:S(2)}, u32[]{:S(2)}) %collective-permute-start.6) | collective-permute-done | bytes 184352 | tf_op jit(solution)/shard_map/ppermute | solution.py:33
  70.3 7.7 %collective-permute-done.7 = bf16[2,2,24,1920]{3,2,1,0:T(8,128)(2,1)S(1)} collective-permute-done((bf16[2,2,24,1920]{3,2,1,0:T(8,128)(2,1)S(1)}, bf16[2,2,24,1920]{3,2,1,0:T(8,128)(2,1)S(1)}, u32[]{:S(2)}, u32[]{:S(2)}) %collective-permute-start.7) | collective-permute-done | bytes 368672 | tf_op jit(solution)/shard_map/ppermute | solution.py:33
  78.8 11.8 %collective-permute-done.19 = bf16[2,2,2,48,768]{4,3,2,1,0:T(8,128)(2,1)S(1)} collective-permute-done((bf16[2,2,2,48,768]{4,3,2,1,0:T(8,128)(2,1)S(1)}, bf16[2,2,2,48,768]{4,3,2,1,0:T(8,128)(2,1)S(1)}, u32[]{:S(2)}, u32[]{:S(2)}) %collective-permute-start.19) | collective-permute-done | bytes 589856 | tf_op jit(solution)/shard_map/ppermute | solution.py:33
  91.6 5.0 collective-permute-done.8
  110.0 5.0 all-gather
  127.0 5.5 multiply_convert_fusion.1
  147.0 10.4 %collective-permute-done.22 = bf16[2,24,1920]{2,1,0:T(8,128)(2,1)S(1)} collective-permute-done((bf16[2,24,1920]{2,1,0:T(8,128)(2,1)S(1)}, bf16[2,24,1920]{2,1,0:T(8,128)(2,1)S(1)}, u32[]{:S(2)}, u32[]{:S(2)}) %collective-permute-start.22) | collective-permute-done | bytes 184352 | tf_op jit(solution)/shard_map/ppermute | solution.py:33
  163.1 7.7 %collective-permute-done.23 = bf16[2,2,24,1920]{3,2,1,0:T(8,128)(2,1)S(1)} collective-permute-done((bf16[2,2,24,1920]{3,2,1,0:T(8,128)(2,1)S(1)}, bf16[2,2,24,1920]{3,2,1,0:T(8,128)(2,1)S(1)}, u32[]{:S(2)}, u32[]{:S(2)}) %collective-permute-start.23) | collective-permute-done | bytes 368672 | tf_op jit(solution)/shard_map/ppermute | solution.py:33
  173.9 9.5 %collective-permute-done.35 = bf16[2,2,2,48,768]{4,3,1,2,0:T(8,128)(2,1)S(1)} collective-permute-done((bf16[2,2,2,48,768]{4,3,1,2,0:T(8,128)(2,1)S(1)}, bf16[2,2,2,48,768]{4,3,1,2,0:T(8,128)(2,1)S(1)}, u32[]{:S(2)}, u32[]{:S(2)}) %collective-permute-start.35) | collective-permute-done | bytes 589856 | tf_op jit(solution)/shard_map/ppermute | solution.py:33
  216.9 5.8 %multiply_convert_fusion = (bf16[256,1792]{1,0:T(8,128)(2,1)S(1)}, f32[256,1792]{1,0:T(8,128)}) fusion(f32[256,1792]{1,0:T(8,128)} %slice.426, f32[1792]{0:T(1024)} %mul.737, f32[3,1792]{1,0:T(4,128)} %collective-permute-done.26, f32[1792]{0:T(1024)} %mul.734, f32[1792]{0:T(1024)} %mul.731, f32[1792]{0:T(1024)} %mul.722, f32[1792]{0:T(1024)} %add.507), kind=kLoop, calls=%fused_computation.98 | loop fusion | flops 7340032 | bytes 4644864 | tf_op jit(solution)/shard_map/convert_element_type | solution.py:313
  233.9 5.0 all-gather.1
  279.7 8.7 %all-gather.11.cloned.1.call-done = bf16[4,24,64,128]{3,2,1,0:T(8,128)(2,1)} async-done(((bf16[1,24,64,128]{3,2,1,0:T(8,128)(2,1)}), bf16[4,24,64,128]{3,2,1,0:T(8,128)(2,1)}) %all-gather.11.cloned.1.call-update) | async-done | bytes 1572880 | tf_op jit(solution)/shard_map/all_gather | solution.py:88
  295.5 9.1 %shard_map.214 = (f32[256,1536]{1,0:T(8,128)S(1)}, f32[256,128]{1,0:T(8,128)S(1)}, f32[256,128]{1,0:T(8,128)S(1)}, f32[256,24]{1,0:T(8,128)S(1)}, f32[24,256]{1,0:T(8,128)S(1)}, /*index=5*/f32[256,128]{1,0:T(8,128)S(1)}) custom-call(bf16[256,1536]{1,0:T(8,128)(2,1)S(1)} %copy-done.21, bf16[256,1536]{1,0:T(8,128)(2,1)S(1)} %copy-done.3, ...), custom_call_target="tpu_custom_call" | custom-call | tf_op jit(solution)/shard_map/pallas_call | solution.py:411
  305.9 5.8 %multiply_reduce_fusion.1 = (f32[1792]{0:T(1024)}, f32[1792]{0:T(1024)}, f32[1792]{0:T(1024)}, f32[1792]{0:T(1024)}, f32[1792]{0:T(1024)S(1)}, /*index=5*/f32[256,1792]{1,0:T(8,128)S(1)}) fusion(f32[256,1792]{1,0:T(8,128)} %slice.426, f32[3,1792]{1,0:T(4,128)} %collective-permute-done.26, f32[256,1920]{1,0:T(8,128)} %copy-done.63, ...), kind=kLoop, calls=%fused_computation.91 | loop fusion | flops 10083584 | bytes 9232384 | tf_op jit(solution)/shard_map/reduce_sum | solution.py:439
  370.3 9.1 %shard_map.216 = (f32[256,1536]{1,0:T(8,128)S(1)}, f32[256,128]{1,0:T(8,128)S(1)}, f32[256,128]{1,0:T(8,128)S(1)}, f32[256,24]{1,0:T(8,128)S(1)}, f32[24,256]{1,0:T(8,128)S(1)}, /*index=5*/f32[256,128]{1,0:T(8,128)S(1)}) custom-call(bf16[256,1536]{1,0:T(8,128)(2,1)S(1)} %copy-done.23, bf16[256,1536]{1,0:T(8,128)(2,1)S(1)} %copy-done.1, ...), custom_call_target="tpu_custom_call" | custom-call | tf_op jit(solution)/shard_map/pallas_call | solution.py:411
  406.6 22.2 %collective-permute-done.62 = f32[3,2,24]{2,0,1:T(4,128)S(1)} collective-permute-done((f32[3,2,24]{2,0,1:T(4,128)S(1)}, f32[3,2,24]{2,0,1:T(4,128)S(1)}, u32[]{:S(2)}, u32[]{:S(2)}) %collective-permute-start.62) | collective-permute-done | bytes 608 | tf_op jit(solution)/shard_map/ppermute | solution.py:33
  446.6 15.5 %collective-permute-done.40 = f32[2,2,2,2,352]{4,3,1,0,2:T(2,128)S(1)} collective-permute-done((f32[2,2,2,2,352]{4,3,1,0,2:T(2,128)S(1)}, f32[2,2,2,2,352]{4,3,1,0,2:T(2,128)S(1)}, u32[]{:S(2)}, u32[]{:S(2)}) %collective-permute-start.40) | collective-permute-done | bytes 22560 | tf_op jit(solution)/shard_map/ppermute | solution.py:33
  481.0 4.8 collective-permute-done.43
  488.3 9.1 %collective-permute-done.56 = bf16[2,2,2,48,768]{4,3,2,0,1:T(8,128)(2,1)} collective-permute-done((bf16[2,2,2,48,768]{4,3,2,0,1:T(8,128)(2,1)S(1)}, bf16[2,2,2,48,768]{4,3,2,0,1:T(8,128)(2,1)}, u32[]{:S(2)}, u32[]{:S(2)}) %collective-permute-start.56) | collective-permute-done | bytes 589856 | tf_op jit(solution)/shard_map/ppermute | solution.py:33
  500.5 6.3 %collective-permute-done.57 = bf16[2,2,48,768]{3,2,1,0:T(8,128)(2,1)S(1)} collective-permute-done((bf16[2,2,48,768]{3,2,1,0:T(8,128)(2,1)S(1)}, bf16[2,2,48,768]{3,2,1,0:T(8,128)(2,1)S(1)}, u32[]{:S(2)}, u32[]{:S(2)}) %collective-permute-start.57) | collective-permute-done | bytes 294944 | tf_op jit(solution)/shard_map/ppermute | solution.py:33
  506.9 13.3 %collective-permute-done.50 = bf16[2,2,2,2,24,1920]{5,4,3,2,0,1:T(8,128)(2,1)} collective-permute-done((bf16[2,2,2,2,24,1920]{5,4,3,2,0,1:T(8,128)(2,1)}, bf16[2,2,2,2,24,1920]{5,4,3,2,0,1:T(8,128)(2,1)}, u32[]{:S(2)}, u32[]{:S(2)}) %collective-permute-start.50) | collective-permute-done | bytes 1474592 | tf_op jit(solution)/shard_map/ppermute | solution.py:33
  525.1 13.8 %collective-permute-done.51 = bf16[2,2,2,24,1920]{4,3,2,1,0:T(8,128)(2,1)S(1)} collective-permute-done((bf16[2,2,2,24,1920]{4,3,2,1,0:T(8,128)(2,1)S(1)}, bf16[2,2,2,24,1920]{4,3,2,1,0:T(8,128)(2,1)S(1)}, u32[]{:S(2)}, u32[]{:S(2)}) %collective-permute-start.51) | collective-permute-done | bytes 737312 | tf_op jit(solution)/shard_map/ppermute | solution.py:33
  540.3 14.5 %collective-permute-done.52 = bf16[2,2,24,1920]{3,2,1,0:T(8,128)(2,1)S(1)} collective-permute-done((bf16[2,2,24,1920]{3,2,1,0:T(8,128)(2,1)S(1)}, bf16[2,2,24,1920]{3,2,1,0:T(8,128)(2,1)S(1)}, u32[]{:S(2)}, u32[]{:S(2)}) %collective-permute-start.52) | collective-permute-done | bytes 368672 | tf_op jit(solution)/shard_map/ppermute | solution.py:33
  555.7 5.1 collective-permute-done.53
  (842 shorter events, 330.3 us)
Async XLA Ops:
  7.2 184.7 %all-gather.7.cloned.1.call-start = ((), (), s32[]{:S(2)}) async-start(), calls=%async_computation | async-start | bytes 1966080 | tf_op jit(solution)/shard_map/all_gather | solution.py:88
  15.3 30.3 %collective-permute-start.16 = (bf16[48,768]{1,0:T(8,128)(2,1)S(1)}, bf16[48,768]{1,0:T(8,128)(2,1)S(1)}, u32[]{:S(2)}, u32[]{:S(2)}) collective-permute-start(bf16[48,768]{1,0:T(8,128)(2,1)S(1)} %get-tuple-element.211), channel_id=1, source_target_pairs={{0,4},{1,5},{2,6},{3,7},{4,0},{5,1},{6,2},{7,3},{8,12},{9,13},{10,... | collective-permute-start | bytes 221192 | tf_op jit(solution)/shard_map/ppermute | solution.py:33
  17.8 25.2 %collective-permute-start.11 = (bf16[24,1536]{1,0:T(8,128)(2,1)S(1)}, bf16[24,1536]{1,0:T(8,128)(2,1)S(1)}, u32[]{:S(2)}, u32[]{:S(2)}) collective-permute-start(bf16[24,1536]{1,0:T(8,128)(2,1)S(1)} %get-tuple-element.191), channel_id=1, source_target_pairs={{0,16},{1,17},{2,18},{3,19},{4,20},{5,21},{6,22},{7,23},{8,24},{9,... | collective-permute-start | bytes 221192 | tf_op jit(solution)/shard_map/ppermute | solution.py:33
  19.8 26.3 %collective-permute-start.5 = (bf16[24,1920]{1,0:T(8,128)(2,1)S(1)}, bf16[24,1920]{1,0:T(8,128)(2,1)S(1)}, u32[]{:S(2)}, u32[]{:S(2)}) collective-permute-start(bf16[24,1920]{1,0:T(8,128)(2,1)S(1)} %fusion.129), channel_id=1, source_target_pairs={{0,2},{1,3},{2,0},{3,1},{4,6},{5,7},{6,4},{7,5},{8,10},{9,11},{10,... | collective-permute-start | bytes 276488 | tf_op jit(solution)/shard_map/ppermute | solution.py:33
  65.4 25.5 %collective-permute-start.14 = (bf16[2,2,2,24,1536]{4,3,2,1,0:T(8,128)(2,1)S(1)}, bf16[2,2,2,24,1536]{4,3,2,1,0:T(8,128)(2,1)S(1)}, u32[]{:S(2)}, u32[]{:S(2)}) collective-permute-start(bf16[2,2,2,24,1536]{4,3,2,1,0:T(8,128)(2,1)S(1)} %pad_maximum_fusion.19), channel_id=1, source_target_pairs={{0,2},{1,3},{2,0},{3,1},{4,6},{5,7},{6,4},{7,5},{8,10},{9,11},{10,... | collective-permute-start | bytes 1769480 | tf_op jit(solution)/shard_map/ppermute | solution.py:33
  107.4 26.7 %collective-permute-start.27 = (bf16[24,1536]{1,0:T(8,128)(2,1)S(1)}, bf16[24,1536]{1,0:T(8,128)(2,1)}, u32[]{:S(2)}, u32[]{:S(2)}) collective-permute-start(bf16[24,1536]{1,0:T(8,128)(2,1)S(1)} %get-tuple-element.55), channel_id=1, source_target_pairs={{0,16},{1,17},{2,18},{3,19},{4,20},{5,21},{6,22},{7,23},{8,24},{9,... | collective-permute-start | bytes 221192 | tf_op jit(solution)/shard_map/ppermute | solution.py:33
  108.0 29.6 %collective-permute-start.32 = (bf16[48,768]{1,0:T(8,128)(2,1)S(1)}, bf16[48,768]{1,0:T(8,128)(2,1)}, u32[]{:S(2)}, u32[]{:S(2)}) collective-permute-start(bf16[48,768]{1,0:T(8,128)(2,1)S(1)} %get-tuple-element.57), channel_id=1, source_target_pairs={{0,4},{1,5},{2,6},{3,7},{4,0},{5,1},{6,2},{7,3},{8,12},{9,13},{10,... | collective-permute-start | bytes 221192 | tf_op jit(solution)/shard_map/ppermute | solution.py:33
  108.5 30.6 %collective-permute-start.21 = (bf16[24,1920]{1,0:T(8,128)(2,1)S(1)}, bf16[24,1920]{1,0:T(8,128)(2,1)S(1)}, u32[]{:S(2)}, u32[]{:S(2)}) collective-permute-start(bf16[24,1920]{1,0:T(8,128)(2,1)S(1)} %fusion.130), channel_id=1, source_target_pairs={{0,2},{1,3},{2,0},{3,1},{4,6},{5,7},{6,4},{7,5},{8,10},{9,11},{10,... | collective-permute-start | bytes 276488 | tf_op jit(solution)/shard_map/ppermute | solution.py:33
  133.8 123.1 %all-gather.9.cloned.1.call-start = ((), (), s32[]{:S(2)}) async-start(), calls=%async_computation.1 | async-start | bytes 1966080 | tf_op jit(solution)/shard_map/all_gather | solution.py:88
  173.9 51.4 %collective-permute-start.31 = (bf16[2,2,2,2,24,1536]{5,4,0,1,2,3:T(8,128)(2,1)}, bf16[2,2,2,2,24,1536]{5,4,0,1,2,3:T(8,128)(2,1)}, u32[]{:S(2)}, u32[]{:S(2)}) collective-permute-start(bf16[2,2,2,2,24,1536]{5,4,0,1,2,3:T(8,128)(2,1)} %pad_maximum_fusion.14), channel_id=1, source_target_pairs={{0,1},{1,0},{2,3},{3,2},{4,5},{5,4},{6,7},{7,6},{8,9},{9,8},{10,11... | collective-permute-start | bytes 3538952 | tf_op jit(solution)/shard_map/ppermute | solution.py:33
  184.7 42.6 %collective-permute-start.36 = (bf16[2,2,2,2,48,768]{5,4,2,3,0,1:T(8,128)(2,1)}, bf16[2,2,2,2,48,768]{5,4,2,3,0,1:T(8,128)(2,1)}, u32[]{:S(2)}, u32[]{:S(2)}) collective-permute-start(bf16[2,2,2,2,48,768]{5,4,2,3,0,1:T(8,128)(2,1)} %pad_maximum_fusion.15), channel_id=1, source_target_pairs={{0,1},{1,0},{2,3},{3,2},{4,5},{5,4},{6,7},{7,6},{8,9},{9,8},{10,11... | collective-permute-start | bytes 3538952 | tf_op jit(solution)/shard_map/ppermute | solution.py:33
  224.8 63.6 %all-gather.11.cloned.1.call-start = ((), (), s32[]{:S(2)}) async-start(), calls=%async_computation.2 | async-start | bytes 1966080 | tf_op jit(solution)/shard_map/all_gather | solution.py:88
  270.2 93.7 %all-gather.13.cloned.1.call-start = ((), (), s32[]{:S(2)}) async-start(), calls=%async_computation.3 | async-start | bytes 1966080 | tf_op jit(solution)/shard_map/all_gather | solution.py:88
  357.6 32.8 %collective-permute-start.54 = (bf16[2,2,2,2,2,48,768]{6,5,4,2,3,0,1:T(8,128)(2,1)}, bf16[2,2,2,2,2,48,768]{6,5,4,2,3,0,1:T(8,128)(2,1)}, u32[]{:S(2)}, u32[]{:S(2)}) collective-permute-start(bf16[2,2,2,2,2,48,768]{6,5,4,2,3,0,1:T(8,128)(2,1)} %bitcast.617), channel_id=1, source_target_pairs={{0,1},{1,0},{2,3},{3,2},{4,5},{5,4},{6,7},{7,6},{8,9},{9,8},{10,11... | collective-permute-start | bytes 7077896 | tf_op jit(solution)/shard_map/ppermute | solution.py:33
  358.9 42.8 %collective-permute-start.44 = (bf16[2,2,2,2,2,24,1536]{6,5,4,0,1,2,3:T(8,128)(2,1)}, bf16[2,2,2,2,2,24,1536]{6,5,4,0,1,2,3:T(8,128)(2,1)}, u32[]{:S(2)}, u32[]{:S(2)}) collective-permute-start(bf16[2,2,2,2,2,24,1536]{6,5,4,0,1,2,3:T(8,128)(2,1)} %bitcast.618), channel_id=1, source_target_pairs={{0,1},{1,0},{2,3},{3,2},{4,5},{5,4},{6,7},{7,6},{8,9},{9,8},{10,11... | collective-permute-start | bytes 7077896 | tf_op jit(solution)/shard_map/ppermute | solution.py:33
  394.4 40.1 %collective-permute-start.38 = (f32[3,1792]{1,0:T(4,128)S(1)}, f32[3,1792]{1,0:T(4,128)S(1)}, u32[]{:S(2)}, u32[]{:S(2)}) collective-permute-start(f32[3,1792]{1,0:T(4,128)S(1)} %slice.461), channel_id=1, source_target_pairs={{1,0},{2,1},{3,2},{5,4},{6,5},{7,6},{9,8},{10,9},{11,10},{13,12},{... | collective-permute-start | bytes 64520 | tf_op jit(solution)/shard_map/ppermute | solution.py:25
  399.7 70.5 %collective-permute-start.55 = (bf16[2,2,2,2,48,768]{5,4,3,1,2,0:T(8,128)(2,1)}, bf16[2,2,2,2,48,768]{5,4,3,1,2,0:T(8,128)(2,1)}, u32[]{:S(2)}, u32[]{:S(2)}) collective-permute-start(bf16[2,2,2,2,48,768]{5,4,3,1,2,0:T(8,128)(2,1)} %dynamic-slice_bitcast_fusion.1), channel_id=1, source_target_pairs={{0,8},{1,9},{2,10},{3,11},{4,12},{5,13},{6,14},{7,15},{8,0},{9,1},... | collective-permute-start | bytes 3538952 | tf_op jit(solution)/shard_map/ppermute | solution.py:33
  401.2 27.6 %collective-permute-start.62 = (f32[3,2,24]{2,0,1:T(4,128)S(1)}, f32[3,2,24]{2,0,1:T(4,128)S(1)}, u32[]{:S(2)}, u32[]{:S(2)}) collective-permute-start(f32[3,2,24]{2,0,1:T(4,128)S(1)} %add.603), channel_id=1, source_target_pairs={{0,8},{1,9},{2,10},{3,11},{4,12},{5,13},{6,14},{7,15},{8,0},{9,1},... | collective-permute-start | bytes 1736 | tf_op jit(solution)/shard_map/ppermute | solution.py:33
  433.8 40.6 %collective-permute-start.45 = (bf16[2,2,2,2,24,1536]{5,4,3,0,1,2:T(8,128)(2,1)}, bf16[2,2,2,2,24,1536]{5,4,3,0,1,2:T(8,128)(2,1)}, u32[]{:S(2)}, u32[]{:S(2)}) collective-permute-start(bf16[2,2,2,2,24,1536]{5,4,3,0,1,2:T(8,128)(2,1)} %dynamic-slice_bitcast_fusion.2), channel_id=1, source_target_pairs={{0,2},{1,3},{2,0},{3,1},{4,6},{5,7},{6,4},{7,5},{8,10},{9,11},{10,... | collective-permute-start | bytes 3538952 | tf_op jit(solution)/shard_map/ppermute | solution.py:33
  444.0 33.5 %collective-permute-start.49 = (bf16[2,2,2,2,2,24,1920]{6,5,4,3,0,1,2:T(8,128)(2,1)S(1)}, bf16[2,2,2,2,2,24,1920]{6,5,4,3,0,1,2:T(8,128)(2,1)S(1)}, u32[]{:S(2)}, u32[]{:S(2)}) collective-permute-start(bf16[2,2,2,2,2,24,1920]{6,5,4,3,0,1,2:T(8,128)(2,1)S(1)} %bitcast.644), channel_id=1, source_target_pairs={{0,1},{1,0},{2,3},{3,2},{4,5},{5,4},{6,7},{7,6},{8,9},{9,8},{10,11... | collective-permute-start | bytes 8847368 | tf_op jit(solution)/shard_map/ppermute | solution.py:33
  472.0 25.4 %collective-permute-start.56 = (bf16[2,2,2,48,768]{4,3,2,0,1:T(8,128)(2,1)S(1)}, bf16[2,2,2,48,768]{4,3,2,0,1:T(8,128)(2,1)}, u32[]{:S(2)}, u32[]{:S(2)}) collective-permute-start(bf16[2,2,2,48,768]{4,3,2,0,1:T(8,128)(2,1)S(1)} %dynamic-slice_bitcast_fusion.4), channel_id=1, source_target_pairs={{0,16},{1,17},{2,18},{3,19},{4,20},{5,21},{6,22},{7,23},{8,24},{9,... | collective-permute-start | bytes 1769480 | tf_op jit(solution)/shard_map/ppermute | solution.py:33
  479.5 40.7 %collective-permute-start.50 = (bf16[2,2,2,2,24,1920]{5,4,3,2,0,1:T(8,128)(2,1)}, bf16[2,2,2,2,24,1920]{5,4,3,2,0,1:T(8,128)(2,1)}, u32[]{:S(2)}, u32[]{:S(2)}) collective-permute-start(bf16[2,2,2,2,24,1920]{5,4,3,2,0,1:T(8,128)(2,1)} %dynamic-slice_bitcast_fusion), channel_id=1, source_target_pairs={{0,4},{1,5},{2,6},{3,7},{4,0},{5,1},{6,2},{7,3},{8,12},{9,13},{10,... | collective-permute-start | bytes 4423688 | tf_op jit(solution)/shard_map/ppermute | solution.py:33
  500.2 24.0 %collective-permute-start.47 = (bf16[2,2,24,1536]{3,2,1,0:T(8,128)(2,1)S(1)}, bf16[2,2,24,1536]{3,2,1,0:T(8,128)(2,1)S(1)}, u32[]{:S(2)}, u32[]{:S(2)}) collective-permute-start(bf16[2,2,24,1536]{3,2,1,0:T(8,128)(2,1)S(1)} %dynamic-slice_bitcast_fusion.8), channel_id=1, source_target_pairs={{0,8},{1,9},{2,10},{3,11},{4,12},{5,13},{6,14},{7,15},{8,0},{9,1},... | collective-permute-start | bytes 884744 | tf_op jit(solution)/shard_map/ppermute | solution.py:33
  523.6 31.4 %collective-permute-start.58 = (bf16[2,48,768]{2,1,0:T(8,128)(2,1)S(1)}, bf16[2,48,768]{2,1,0:T(8,128)(2,1)S(1)}, u32[]{:S(2)}, u32[]{:S(2)}) collective-permute-start(bf16[2,48,768]{2,1,0:T(8,128)(2,1)S(1)} %dynamic-slice_bitcast_fusion.10), channel_id=1, source_target_pairs={{0,4},{1,5},{2,6},{3,7},{4,0},{5,1},{6,2},{7,3},{8,12},{9,13},{10,... | collective-permute-start | bytes 442376 | tf_op jit(solution)/shard_map/ppermute | solution.py:33
  (246 other events, 2084.8 us)
Sparse Core Ops, SparseCore 0:
  134.0 20.3 all-gather.6
  224.9 18.1 all-gather.8
  270.3 18.0 all-gather.10
  332.6 21.5 all-gather.12
